TPU v7x, 128 devices: a whole 4x4x4 slice. The times are simulated.
128 devices in a mesh: seq: 8 (over x, y_lo), tensor: 8 (over z, core), pool: 2 (over y_hi).
Axes of the slice: x: 4, y: 4 (y_hi: 2, y_lo: 2; y = y_hi * 2 + y_lo), z: 4, core: 2. Of those that a mesh axis runs over, the one named last changes fastest.
Arguments:
- pre_x: bfloat16 [8192, 8192], P(('seq', 'pool')), may hold values from -6 to 6
- w_query: bfloat16 [8192, 8192], P(None, 'tensor'), may hold values from -4 to 4
- w_key: bfloat16 [8192, 1024], P(None, 'tensor'), may hold values from -4 to 4
- w_value: bfloat16 [8192, 1024], P(None, 'tensor'), may hold values from -0.0625 to 0.0625
- dec_x: bfloat16 [4, 128, 8192], P(None, ('seq', 'pool'), 'tensor'), may hold values from -6 to 6
- cache: bfloat16 [2048, 16, 2, 1024], P(('seq', 'pool'), None, None, 'tensor'), may hold values from -6 to 6
- lengths: int32 [128], P(('seq', 'pool')), may hold values from 64 to 256, as said below
- page_table: int32 [128, 16], P(('seq', 'pool')), may hold values from 0 to 127, as said below
- dest_slots: int32 [16, 32], P(('seq', 'pool')), may hold values from 0 to 127, as said below
Outputs:
- pre_out: bfloat16 [8192, 8192], P(('seq', 'pool'), 'tensor')
- dec_out: bfloat16 [4, 128, 8192], P(None, ('seq', 'pool'), 'tensor')
Inputs may be any that keep to these rules, and one draw needn't show every extreme that they name: `lengths`: every group of 8 rows has a row with the most. `page_table`: rows g * 8 to (g + 1) * 8 - 1 name pages of group g's pool; each of the group's 128 pages is named exactly once in the group's table. `dest_slots`: the slots of a group are distinct, and each is a page that the group's page table names within the live tokens of its row.
All inputs are finite; a program needn't handle non-finite values.
Results may differ from a plain program's by a relative error of at most 0.019.
Values may be sent and summed in bfloat16 or wider, within the bound.
A program may use at most 128 MiB of HBM per device.

v0:
```python
import math

import jax
import jax.numpy as jnp
from jax import lax
from jax.sharding import PartitionSpec as P

KVH = 8
HD = 128
QH = 64
PAGE = 16


def per_device(pre_x, w_query, w_key, w_value, dec_x, cache, lengths, page_table, dest_slots):
    groups = lax.axis_size(("seq", "pool"))
    my_group = lax.axis_index(("seq", "pool"))
    token_count = pre_x.shape[0]
    kv_local = w_key.shape[1] // HD
    share = QH // KVH
    score_scale = HD ** (-0.5)
    queries = jnp.dot(pre_x, w_query, preferred_element_type=jnp.float32).astype(jnp.bfloat16)
    queries = queries.reshape(token_count, kv_local, share, HD)
    key_rows = jnp.dot(pre_x, w_key, preferred_element_type=jnp.float32).astype(jnp.bfloat16)
    value_rows = jnp.dot(pre_x, w_value, preferred_element_type=jnp.float32).astype(jnp.bfloat16)
    packed = jnp.stack([key_rows, value_rows], axis=1)
    query_first = my_group * token_count
    query_last = query_first + token_count - 1
    query_pos = query_first + jnp.arange(token_count, dtype=jnp.int32)
    initial = (
        jnp.full((kv_local, share, token_count), -1e30, jnp.float32),
        jnp.zeros((kv_local, share, token_count), jnp.float32),
        jnp.zeros((kv_local, share, token_count, HD), jnp.float32),
    )

    def absorb(running, kv_block, key_pos):
        largest, totals, weighted = running
        width = kv_block.shape[0]
        block_keys = kv_block[:, 0].reshape(width, kv_local, HD)
        block_values = kv_block[:, 1].reshape(width, kv_local, HD)
        scores = (
            jnp.einsum("thgd,khd->hgtk", queries, block_keys, preferred_element_type=jnp.float32)
            * score_scale
        )
        allowed = key_pos[None, :] <= query_pos[:, None]
        scores = jnp.where(allowed, scores, -1e30)
        updated = jnp.maximum(largest, jnp.max(scores, axis=-1))
        rescale = jnp.exp(largest - updated)
        weights = jnp.where(allowed, jnp.exp(scores - updated[..., None]), 0.0)
        totals = totals * rescale + jnp.sum(weights, axis=-1)
        weighted = weighted * rescale[..., None] + jnp.einsum(
            "hgtk,khd->hgtd",
            weights.astype(jnp.bfloat16),
            block_values,
            preferred_element_type=jnp.float32,
        )
        return (updated, totals, weighted)

    kv_piece = lax.all_gather(packed, ("seq", "pool"), axis=0, tiled=True)
    width = kv_piece.shape[0]
    block_size = math.gcd(width, 512)
    count = width // block_size

    def one_block(index, inner):
        offset = (index * block_size).astype(jnp.int32)
        kv_block = lax.dynamic_slice_in_dim(kv_piece, offset, block_size, 0)
        key_pos = offset + jnp.arange(block_size, dtype=jnp.int32)
        needed = (offset >= 0) & (offset <= query_last)
        return lax.cond(
            needed, lambda carry: absorb(carry, kv_block, key_pos), lambda carry: carry, inner
        )

    running = lax.fori_loop(0, count, one_block, initial)
    largest, totals, weighted = running
    pre_out = (
        (weighted / totals[..., None])
        .transpose(2, 0, 1, 3)
        .reshape(token_count, -1)
        .astype(jnp.bfloat16)
    )
    per_group = token_count // (PAGE * groups)
    page_blocks = packed.reshape(groups * per_group, PAGE, 2, kv_local * HD)
    arrived = lax.all_to_all(page_blocks, ("seq", "pool"), split_axis=0, concat_axis=0, tiled=True)
    pool_pages = cache.at[dest_slots[0]].set(arrived)
    step_x = lax.all_gather(dec_x, "tensor", axis=2, tiled=True)
    n_steps = step_x.shape[0]
    n_rows = step_x.shape[1]
    flat_x = step_x.reshape(n_steps * n_rows, -1)
    dec_query = jnp.dot(flat_x, w_query, preferred_element_type=jnp.float32).astype(jnp.bfloat16)
    dec_query = dec_query.reshape(n_steps, n_rows, kv_local, share, HD)
    dec_keys = jnp.dot(flat_x, w_key, preferred_element_type=jnp.float32).astype(jnp.bfloat16)
    dec_keys = dec_keys.reshape(n_steps, n_rows, kv_local, HD)
    dec_values = jnp.dot(flat_x, w_value, preferred_element_type=jnp.float32).astype(jnp.bfloat16)
    dec_values = dec_values.reshape(n_steps, n_rows, kv_local, HD)
    context = pool_pages[page_table].reshape(n_rows, -1, 2, kv_local, HD)
    context_keys = context[:, :, 0]
    context_values = context[:, :, 1]
    live = jnp.arange(context.shape[1], dtype=jnp.int32)[None, :] < lengths[:, None]
    live_mask = live[None, :, None, None, :]
    old_scores = (
        jnp.einsum("srhgd,rkhd->srhgk", dec_query, context_keys, preferred_element_type=jnp.float32)
        * score_scale
    )
    old_scores = jnp.where(live_mask, old_scores, -1e30)
    causal = (
        jnp.arange(n_steps, dtype=jnp.int32)[None, :]
        <= jnp.arange(n_steps, dtype=jnp.int32)[:, None]
    )
    causal_mask = causal[:, None, None, None, :]
    new_scores = (
        jnp.einsum("srhgd,trhd->srhgt", dec_query, dec_keys, preferred_element_type=jnp.float32)
        * score_scale
    )
    new_scores = jnp.where(causal_mask, new_scores, -1e30)
    highest = jnp.maximum(jnp.max(old_scores, axis=-1), jnp.max(new_scores, axis=-1))
    old_weights = jnp.where(live_mask, jnp.exp(old_scores - highest[..., None]), 0.0)
    new_weights = jnp.where(causal_mask, jnp.exp(new_scores - highest[..., None]), 0.0)
    step_totals = jnp.sum(old_weights, axis=-1) + jnp.sum(new_weights, axis=-1)
    mixed = jnp.einsum(
        "srhgk,rkhd->srhgd",
        old_weights.astype(jnp.bfloat16),
        context_values,
        preferred_element_type=jnp.float32,
    )
    mixed = mixed + jnp.einsum(
        "srhgt,trhd->srhgd",
        new_weights.astype(jnp.bfloat16),
        dec_values,
        preferred_element_type=jnp.float32,
    )
    dec_out = (mixed / step_totals[..., None]).reshape(n_steps, n_rows, -1).astype(jnp.bfloat16)
    return (pre_out, dec_out)


def solution(mesh):
    in_specs = (
        P(("seq", "pool"), None),
        P(None, "tensor"),
        P(None, "tensor"),
        P(None, "tensor"),
        P(None, ("seq", "pool"), "tensor"),
        P(("seq", "pool"), None, None, "tensor"),
        P(("seq", "pool")),
        P(("seq", "pool"), None),
        P(("seq", "pool"), None),
    )
    out_specs = (P(("seq", "pool"), "tensor"), P(None, ("seq", "pool"), "tensor"))
    return jax.shard_map(
        per_device, mesh=mesh, in_specs=in_specs, out_specs=out_specs, check_vma=False
    )
```

profile of v0, /device:TPU:30, one launch (start us, length us, event | category | flops | bytes accessed | tf_op | source)
XLA Modules:
  0.0 275.7 jit_solution(18351319657254984612)
XLA Ops:
  7.2 3.1 %copy.69 = bf16[128,16,2,128]{3,2,1,0:T(2,128)(2,1)} copy(bf16[128,16,2,128]{3,2,1,0:T(2,128)(2,1)} %param.18) | data formatting | bytes 2097152
  10.3 6.5 %convolution_convert_fusion.2 = bf16[512,128]{1,0:T(8,128)(2,1)S(1)} fusion(bf16[512,8192]{1,0:T(8,128)(2,1)} %param.13, bf16[8192,128]{1,0:T(8,128)(2,1)S(1)} %copy-done), kind=kOutput, calls=%fused_computation.34 | convolution fusion | flops 1073807360 | bytes 10616832 | tf_op jit(solution)/shard_map/dot_general | solution.py:23
  21.7 7.1 %all-to-all-start = ((bf16[32,16,2,128]{3,2,1,0:T(2,128)(2,1)}), bf16[32,16,2,128]{3,2,1,0:T(2,128)(2,1)S(1)}, u32[]{:S(2)}, u32[]{:S(2)}) async-start(bf16[32,16,2,128]{3,2,1,0:T(2,128)(2,1)} %pad_maximum_fusion.1), calls=%async_computation | async-start | bytes 524288 | tf_op jit(solution)/shard_map/all_to_all | solution.py:82
  29.5 14.5 %all_gather.7 = bf16[4,8,8192]{2,1,0:T(8,128)(2,1)S(1)} all-gather(bf16[4,8,1024]{2,1,0:T(8,128)(2,1)S(1)} %copy-done.5), channel_id=1, replica_groups=mesh['seq'=8,'tensor'=8,'pool'=2] {'tensor'}, dimensions={2}, use_global_device_ids=true | all-gather | bytes 589824 | tf_op jit(solution)/shard_map/all_gather | solution.py:84
  44.5 9.2 %fusion.26 = bf16[4,8,8,128]{3,1,2,0:T(8,128)(2,1)S(1)} fusion(bf16[8192,1024]{1,0:T(8,128)(2,1)} %param.14, bf16[4,8,8192]{2,1,0:T(8,128)(2,1)S(1)} %all_gather.7), kind=kOutput, calls=%fused_computation.42 | convolution fusion | flops 536903680 | bytes 17367040 | tf_op jit(solution)/shard_map/dot_general | solution.py:88
  54.8 12.5 %fusion.19 = bf16[64,8,8,128]{3,1,2,0:T(8,128)(2,1)S(1)} fusion(bf16[512,8192]{1,0:T(8,128)(2,1)S(1)} %bitcast.158, bf16[8192,1024]{1,0:T(8,128)(2,1)} %param.14), kind=kOutput, calls=%fused_computation.30 | convolution fusion | flops 8590458880 | bytes 26214400 | tf_op jit(solution)/shard_map/dot_general | solution.py:21
  70.0 4.4 %scatter_fusion = bf16[128,16,2,128]{3,2,1,0:T(2,128)(2,1)} fusion(bf16[128,16,2,128]{3,2,1,0:T(2,128)(2,1)} %copy.69, s32[32]{0:T(128)} %fusion.54, bf16[32,16,2,128]{3,2,1,0:T(2,128)(2,1)S(1)} %all-to-all-done), kind=kCustom, calls=%fused_computation.1 | custom fusion | bytes 786560 | tf_op jit(solution)/shard_map/scatter | solution.py:83
  74.4 4.8 %gather_fusion = bf16[128,16,2,128]{3,2,1,0:T(2,128)(2,1)} fusion(bf16[128,16,2,128]{3,2,1,0:T(2,128)(2,1)} %scatter_fusion, s32[1024]{0:T(1024)S(1)} %pad_clamp_fusion), kind=kCustom, calls=%fused_computation | custom fusion | bytes 2097664 | tf_op jit(solution)/shard_map/gather | solution.py:94
  84.6 34.8 %all-gather.2.cloned.1.call-done = bf16[8192,2,128]{2,0,1:T(8,128)(2,1)} async-done(((bf16[512,2,128]{2,0,1:T(8,128)(2,1)}), bf16[8192,2,128]{2,0,1:T(8,128)(2,1)}) %all-gather.2.cloned.1.call-update) | async-done | bytes 4194320 | tf_op jit(solution)/shard_map/all_gather | solution.py:58
  120.9 144.1 %while.18 = (s32[]{:T(128)}, f32[1,8,512]{2,1,0:T(8,128)S(1)}, f32[1,8,512]{2,1,0:T(8,128)S(1)}, f32[1,8,512,128]{3,2,1,0:T(8,128)}, s32[]{:T(128)}, /*index=5*/...) while((s32[]{:T(128)}, f32[1,8,512]{2,1,0:T(8,128)S(1)}, ...), condition=%wide.region_5.6_spmd.clone, body=%wide.region_0.5_spmd.clone.sunk | while | flops 1102328832 | bytes 48773520 | solution.py:72
  120.9 8.9 %conditional.3 = ((f32[1,8,512]{2,1,0:T(8,128)S(1)}, f32[1,8,512]{2,1,0:T(8,128)S(1)}, f32[1,8,512,128]{3,2,1,0:T(8,128)})) conditional(s32[]{:T(128)} %convert_element_type.97, (f32[1,8,512]{2,1,0:T(8,128)S(1)}, f32[1,8,512]{2,1,0:T(8,128)S(1)}, f32[1,8,512,128]{3,2,1,0:T(8,128)}) %tuple.56, (s32[]{:T(128)}, s32[512]{0:T(512)S(1)}, s32[]{:T(128)}, ...), branch_computations={%region_1.0_spmd, %region_2.4_spmd} | conditional | flops 1102328832 | bytes 48771228 | solution.py:68
  123.7 4.0 %bitcast_add_fusion = f32[1,8,512,128]{3,2,1,0:T(8,128)S(1)} fusion(f32[1,8,512,128]{3,2,1,0:T(8,128)S(1)} %copy-done.2, f32[512,512,8]{1,0,2:T(8,128)S(1)} %get-tuple-element.274, f32[8,512]{1,0:T(8,128)S(1)} %bitcast.145, pred[512,512]{0,1:T(8,128)(4,1)S(1)} %broadcast_compare_fusion, f32[8,512]{1,0:T(8,128)S(1)} %get-tuple-element.271, ...), kind=kOutput, calls=%fused_computation.11 | convolution fusion | flops 548405248 | bytes 13008904 | tf_op jit(solution)/shard_map/while/body/eval_jaxpr/cond/branch_1_fun/hgtk,khd->hgtd/dot_general | solution.py:50
  129.8 9.0 %conditional.3 = ((f32[1,8,512]{2,1,0:T(8,128)S(1)}, f32[1,8,512]{2,1,0:T(8,128)S(1)}, f32[1,8,512,128]{3,2,1,0:T(8,128)})) conditional(s32[]{:T(128)} %convert_element_type.97, (f32[1,8,512]{2,1,0:T(8,128)S(1)}, f32[1,8,512]{2,1,0:T(8,128)S(1)}, f32[1,8,512,128]{3,2,1,0:T(8,128)}) %tuple.56, (s32[]{:T(128)}, s32[512]{0:T(512)S(1)}, s32[]{:T(128)}, ...), branch_computations={%region_1.0_spmd, %region_2.4_spmd} | conditional | flops 1102328832 | bytes 48771228 | solution.py:68
  130.1 2.5 fusion.2
  132.7 4.0 %bitcast_add_fusion = f32[1,8,512,128]{3,2,1,0:T(8,128)S(1)} fusion(f32[1,8,512,128]{3,2,1,0:T(8,128)S(1)} %copy-done.2, f32[512,512,8]{1,0,2:T(8,128)S(1)} %get-tuple-element.274, f32[8,512]{1,0:T(8,128)S(1)} %bitcast.145, pred[512,512]{0,1:T(8,128)(4,1)S(1)} %broadcast_compare_fusion, f32[8,512]{1,0:T(8,128)S(1)} %get-tuple-element.271, ...), kind=kOutput, calls=%fused_computation.11 | convolution fusion | flops 548405248 | bytes 13008904 | tf_op jit(solution)/shard_map/while/body/eval_jaxpr/cond/branch_1_fun/hgtk,khd->hgtd/dot_general | solution.py:50
  138.8 9.0 %conditional.3 = ((f32[1,8,512]{2,1,0:T(8,128)S(1)}, f32[1,8,512]{2,1,0:T(8,128)S(1)}, f32[1,8,512,128]{3,2,1,0:T(8,128)})) conditional(s32[]{:T(128)} %convert_element_type.97, (f32[1,8,512]{2,1,0:T(8,128)S(1)}, f32[1,8,512]{2,1,0:T(8,128)S(1)}, f32[1,8,512,128]{3,2,1,0:T(8,128)}) %tuple.56, (s32[]{:T(128)}, s32[512]{0:T(512)S(1)}, s32[]{:T(128)}, ...), branch_computations={%region_1.0_spmd, %region_2.4_spmd} | conditional | flops 1102328832 | bytes 48771228 | solution.py:68
  139.1 2.5 fusion.2
  141.7 4.0 %bitcast_add_fusion = f32[1,8,512,128]{3,2,1,0:T(8,128)S(1)} fusion(f32[1,8,512,128]{3,2,1,0:T(8,128)S(1)} %copy-done.2, f32[512,512,8]{1,0,2:T(8,128)S(1)} %get-tuple-element.274, f32[8,512]{1,0:T(8,128)S(1)} %bitcast.145, pred[512,512]{0,1:T(8,128)(4,1)S(1)} %broadcast_compare_fusion, f32[8,512]{1,0:T(8,128)S(1)} %get-tuple-element.271, ...), kind=kOutput, calls=%fused_computation.11 | convolution fusion | flops 548405248 | bytes 13008904 | tf_op jit(solution)/shard_map/while/body/eval_jaxpr/cond/branch_1_fun/hgtk,khd->hgtd/dot_general | solution.py:50
  147.8 9.0 %conditional.3 = ((f32[1,8,512]{2,1,0:T(8,128)S(1)}, f32[1,8,512]{2,1,0:T(8,128)S(1)}, f32[1,8,512,128]{3,2,1,0:T(8,128)})) conditional(s32[]{:T(128)} %convert_element_type.97, (f32[1,8,512]{2,1,0:T(8,128)S(1)}, f32[1,8,512]{2,1,0:T(8,128)S(1)}, f32[1,8,512,128]{3,2,1,0:T(8,128)}) %tuple.56, (s32[]{:T(128)}, s32[512]{0:T(512)S(1)}, s32[]{:T(128)}, ...), branch_computations={%region_1.0_spmd, %region_2.4_spmd} | conditional | flops 1102328832 | bytes 48771228 | solution.py:68
  148.1 2.5 fusion.2
  150.7 4.0 %bitcast_add_fusion = f32[1,8,512,128]{3,2,1,0:T(8,128)S(1)} fusion(f32[1,8,512,128]{3,2,1,0:T(8,128)S(1)} %copy-done.2, f32[512,512,8]{1,0,2:T(8,128)S(1)} %get-tuple-element.274, f32[8,512]{1,0:T(8,128)S(1)} %bitcast.145, pred[512,512]{0,1:T(8,128)(4,1)S(1)} %broadcast_compare_fusion, f32[8,512]{1,0:T(8,128)S(1)} %get-tuple-element.271, ...), kind=kOutput, calls=%fused_computation.11 | convolution fusion | flops 548405248 | bytes 13008904 | tf_op jit(solution)/shard_map/while/body/eval_jaxpr/cond/branch_1_fun/hgtk,khd->hgtd/dot_general | solution.py:50
  156.9 9.0 %conditional.3 = ((f32[1,8,512]{2,1,0:T(8,128)S(1)}, f32[1,8,512]{2,1,0:T(8,128)S(1)}, f32[1,8,512,128]{3,2,1,0:T(8,128)})) conditional(s32[]{:T(128)} %convert_element_type.97, (f32[1,8,512]{2,1,0:T(8,128)S(1)}, f32[1,8,512]{2,1,0:T(8,128)S(1)}, f32[1,8,512,128]{3,2,1,0:T(8,128)}) %tuple.56, (s32[]{:T(128)}, s32[512]{0:T(512)S(1)}, s32[]{:T(128)}, ...), branch_computations={%region_1.0_spmd, %region_2.4_spmd} | conditional | flops 1102328832 | bytes 48771228 | solution.py:68
  157.1 2.5 fusion.2
  159.7 4.0 %bitcast_add_fusion = f32[1,8,512,128]{3,2,1,0:T(8,128)S(1)} fusion(f32[1,8,512,128]{3,2,1,0:T(8,128)S(1)} %copy-done.2, f32[512,512,8]{1,0,2:T(8,128)S(1)} %get-tuple-element.274, f32[8,512]{1,0:T(8,128)S(1)} %bitcast.145, pred[512,512]{0,1:T(8,128)(4,1)S(1)} %broadcast_compare_fusion, f32[8,512]{1,0:T(8,128)S(1)} %get-tuple-element.271, ...), kind=kOutput, calls=%fused_computation.11 | convolution fusion | flops 548405248 | bytes 13008904 | tf_op jit(solution)/shard_map/while/body/eval_jaxpr/cond/branch_1_fun/hgtk,khd->hgtd/dot_general | solution.py:50
  165.9 9.0 %conditional.3 = ((f32[1,8,512]{2,1,0:T(8,128)S(1)}, f32[1,8,512]{2,1,0:T(8,128)S(1)}, f32[1,8,512,128]{3,2,1,0:T(8,128)})) conditional(s32[]{:T(128)} %convert_element_type.97, (f32[1,8,512]{2,1,0:T(8,128)S(1)}, f32[1,8,512]{2,1,0:T(8,128)S(1)}, f32[1,8,512,128]{3,2,1,0:T(8,128)}) %tuple.56, (s32[]{:T(128)}, s32[512]{0:T(512)S(1)}, s32[]{:T(128)}, ...), branch_computations={%region_1.0_spmd, %region_2.4_spmd} | conditional | flops 1102328832 | bytes 48771228 | solution.py:68
  168.7 4.0 %bitcast_add_fusion = f32[1,8,512,128]{3,2,1,0:T(8,128)S(1)} fusion(f32[1,8,512,128]{3,2,1,0:T(8,128)S(1)} %copy-done.2, f32[512,512,8]{1,0,2:T(8,128)S(1)} %get-tuple-element.274, f32[8,512]{1,0:T(8,128)S(1)} %bitcast.145, pred[512,512]{0,1:T(8,128)(4,1)S(1)} %broadcast_compare_fusion, f32[8,512]{1,0:T(8,128)S(1)} %get-tuple-element.271, ...), kind=kOutput, calls=%fused_computation.11 | convolution fusion | flops 548405248 | bytes 13008904 | tf_op jit(solution)/shard_map/while/body/eval_jaxpr/cond/branch_1_fun/hgtk,khd->hgtd/dot_general | solution.py:50
  174.9 9.0 %conditional.3 = ((f32[1,8,512]{2,1,0:T(8,128)S(1)}, f32[1,8,512]{2,1,0:T(8,128)S(1)}, f32[1,8,512,128]{3,2,1,0:T(8,128)})) conditional(s32[]{:T(128)} %convert_element_type.97, (f32[1,8,512]{2,1,0:T(8,128)S(1)}, f32[1,8,512]{2,1,0:T(8,128)S(1)}, f32[1,8,512,128]{3,2,1,0:T(8,128)}) %tuple.56, (s32[]{:T(128)}, s32[512]{0:T(512)S(1)}, s32[]{:T(128)}, ...), branch_computations={%region_1.0_spmd, %region_2.4_spmd} | conditional | flops 1102328832 | bytes 48771228 | solution.py:68
  177.7 4.0 %bitcast_add_fusion = f32[1,8,512,128]{3,2,1,0:T(8,128)S(1)} fusion(f32[1,8,512,128]{3,2,1,0:T(8,128)S(1)} %copy-done.2, f32[512,512,8]{1,0,2:T(8,128)S(1)} %get-tuple-element.274, f32[8,512]{1,0:T(8,128)S(1)} %bitcast.145, pred[512,512]{0,1:T(8,128)(4,1)S(1)} %broadcast_compare_fusion, f32[8,512]{1,0:T(8,128)S(1)} %get-tuple-element.271, ...), kind=kOutput, calls=%fused_computation.11 | convolution fusion | flops 548405248 | bytes 13008904 | tf_op jit(solution)/shard_map/while/body/eval_jaxpr/cond/branch_1_fun/hgtk,khd->hgtd/dot_general | solution.py:50
  183.9 9.0 %conditional.3 = ((f32[1,8,512]{2,1,0:T(8,128)S(1)}, f32[1,8,512]{2,1,0:T(8,128)S(1)}, f32[1,8,512,128]{3,2,1,0:T(8,128)})) conditional(s32[]{:T(128)} %convert_element_type.97, (f32[1,8,512]{2,1,0:T(8,128)S(1)}, f32[1,8,512]{2,1,0:T(8,128)S(1)}, f32[1,8,512,128]{3,2,1,0:T(8,128)}) %tuple.56, (s32[]{:T(128)}, s32[512]{0:T(512)S(1)}, s32[]{:T(128)}, ...), branch_computations={%region_1.0_spmd, %region_2.4_spmd} | conditional | flops 1102328832 | bytes 48771228 | solution.py:68
  184.2 2.5 fusion.2
  186.7 4.0 %bitcast_add_fusion = f32[1,8,512,128]{3,2,1,0:T(8,128)S(1)} fusion(f32[1,8,512,128]{3,2,1,0:T(8,128)S(1)} %copy-done.2, f32[512,512,8]{1,0,2:T(8,128)S(1)} %get-tuple-element.274, f32[8,512]{1,0:T(8,128)S(1)} %bitcast.145, pred[512,512]{0,1:T(8,128)(4,1)S(1)} %broadcast_compare_fusion, f32[8,512]{1,0:T(8,128)S(1)} %get-tuple-element.271, ...), kind=kOutput, calls=%fused_computation.11 | convolution fusion | flops 548405248 | bytes 13008904 | tf_op jit(solution)/shard_map/while/body/eval_jaxpr/cond/branch_1_fun/hgtk,khd->hgtd/dot_general | solution.py:50
  192.9 9.0 %conditional.3 = ((f32[1,8,512]{2,1,0:T(8,128)S(1)}, f32[1,8,512]{2,1,0:T(8,128)S(1)}, f32[1,8,512,128]{3,2,1,0:T(8,128)})) conditional(s32[]{:T(128)} %convert_element_type.97, (f32[1,8,512]{2,1,0:T(8,128)S(1)}, f32[1,8,512]{2,1,0:T(8,128)S(1)}, f32[1,8,512,128]{3,2,1,0:T(8,128)}) %tuple.56, (s32[]{:T(128)}, s32[512]{0:T(512)S(1)}, s32[]{:T(128)}, ...), branch_computations={%region_1.0_spmd, %region_2.4_spmd} | conditional | flops 1102328832 | bytes 48771228 | solution.py:68
  195.7 4.0 %bitcast_add_fusion = f32[1,8,512,128]{3,2,1,0:T(8,128)S(1)} fusion(f32[1,8,512,128]{3,2,1,0:T(8,128)S(1)} %copy-done.2, f32[512,512,8]{1,0,2:T(8,128)S(1)} %get-tuple-element.274, f32[8,512]{1,0:T(8,128)S(1)} %bitcast.145, pred[512,512]{0,1:T(8,128)(4,1)S(1)} %broadcast_compare_fusion, f32[8,512]{1,0:T(8,128)S(1)} %get-tuple-element.271, ...), kind=kOutput, calls=%fused_computation.11 | convolution fusion | flops 548405248 | bytes 13008904 | tf_op jit(solution)/shard_map/while/body/eval_jaxpr/cond/branch_1_fun/hgtk,khd->hgtd/dot_general | solution.py:50
  201.9 9.0 %conditional.3 = ((f32[1,8,512]{2,1,0:T(8,128)S(1)}, f32[1,8,512]{2,1,0:T(8,128)S(1)}, f32[1,8,512,128]{3,2,1,0:T(8,128)})) conditional(s32[]{:T(128)} %convert_element_type.97, (f32[1,8,512]{2,1,0:T(8,128)S(1)}, f32[1,8,512]{2,1,0:T(8,128)S(1)}, f32[1,8,512,128]{3,2,1,0:T(8,128)}) %tuple.56, (s32[]{:T(128)}, s32[512]{0:T(512)S(1)}, s32[]{:T(128)}, ...), branch_computations={%region_1.0_spmd, %region_2.4_spmd} | conditional | flops 1102328832 | bytes 48771228 | solution.py:68
  204.8 4.0 %bitcast_add_fusion = f32[1,8,512,128]{3,2,1,0:T(8,128)S(1)} fusion(f32[1,8,512,128]{3,2,1,0:T(8,128)S(1)} %copy-done.2, f32[512,512,8]{1,0,2:T(8,128)S(1)} %get-tuple-element.274, f32[8,512]{1,0:T(8,128)S(1)} %bitcast.145, pred[512,512]{0,1:T(8,128)(4,1)S(1)} %broadcast_compare_fusion, f32[8,512]{1,0:T(8,128)S(1)} %get-tuple-element.271, ...), kind=kOutput, calls=%fused_computation.11 | convolution fusion | flops 548405248 | bytes 13008904 | tf_op jit(solution)/shard_map/while/body/eval_jaxpr/cond/branch_1_fun/hgtk,khd->hgtd/dot_general | solution.py:50
  210.9 9.0 %conditional.3 = ((f32[1,8,512]{2,1,0:T(8,128)S(1)}, f32[1,8,512]{2,1,0:T(8,128)S(1)}, f32[1,8,512,128]{3,2,1,0:T(8,128)})) conditional(s32[]{:T(128)} %convert_element_type.97, (f32[1,8,512]{2,1,0:T(8,128)S(1)}, f32[1,8,512]{2,1,0:T(8,128)S(1)}, f32[1,8,512,128]{3,2,1,0:T(8,128)}) %tuple.56, (s32[]{:T(128)}, s32[512]{0:T(512)S(1)}, s32[]{:T(128)}, ...), branch_computations={%region_1.0_spmd, %region_2.4_spmd} | conditional | flops 1102328832 | bytes 48771228 | solution.py:68
  213.8 4.0 %bitcast_add_fusion = f32[1,8,512,128]{3,2,1,0:T(8,128)S(1)} fusion(f32[1,8,512,128]{3,2,1,0:T(8,128)S(1)} %copy-done.2, f32[512,512,8]{1,0,2:T(8,128)S(1)} %get-tuple-element.274, f32[8,512]{1,0:T(8,128)S(1)} %bitcast.145, pred[512,512]{0,1:T(8,128)(4,1)S(1)} %broadcast_compare_fusion, f32[8,512]{1,0:T(8,128)S(1)} %get-tuple-element.271, ...), kind=kOutput, calls=%fused_computation.11 | convolution fusion | flops 548405248 | bytes 13008904 | tf_op jit(solution)/shard_map/while/body/eval_jaxpr/cond/branch_1_fun/hgtk,khd->hgtd/dot_general | solution.py:50
  219.9 9.0 %conditional.3 = ((f32[1,8,512]{2,1,0:T(8,128)S(1)}, f32[1,8,512]{2,1,0:T(8,128)S(1)}, f32[1,8,512,128]{3,2,1,0:T(8,128)})) conditional(s32[]{:T(128)} %convert_element_type.97, (f32[1,8,512]{2,1,0:T(8,128)S(1)}, f32[1,8,512]{2,1,0:T(8,128)S(1)}, f32[1,8,512,128]{3,2,1,0:T(8,128)}) %tuple.56, (s32[]{:T(128)}, s32[512]{0:T(512)S(1)}, s32[]{:T(128)}, ...), branch_computations={%region_1.0_spmd, %region_2.4_spmd} | conditional | flops 1102328832 | bytes 48771228 | solution.py:68
  222.8 4.0 %bitcast_add_fusion = f32[1,8,512,128]{3,2,1,0:T(8,128)S(1)} fusion(f32[1,8,512,128]{3,2,1,0:T(8,128)S(1)} %copy-done.2, f32[512,512,8]{1,0,2:T(8,128)S(1)} %get-tuple-element.274, f32[8,512]{1,0:T(8,128)S(1)} %bitcast.145, pred[512,512]{0,1:T(8,128)(4,1)S(1)} %broadcast_compare_fusion, f32[8,512]{1,0:T(8,128)S(1)} %get-tuple-element.271, ...), kind=kOutput, calls=%fused_computation.11 | convolution fusion | flops 548405248 | bytes 13008904 | tf_op jit(solution)/shard_map/while/body/eval_jaxpr/cond/branch_1_fun/hgtk,khd->hgtd/dot_general | solution.py:50
  228.9 9.0 %conditional.3 = ((f32[1,8,512]{2,1,0:T(8,128)S(1)}, f32[1,8,512]{2,1,0:T(8,128)S(1)}, f32[1,8,512,128]{3,2,1,0:T(8,128)})) conditional(s32[]{:T(128)} %convert_element_type.97, (f32[1,8,512]{2,1,0:T(8,128)S(1)}, f32[1,8,512]{2,1,0:T(8,128)S(1)}, f32[1,8,512,128]{3,2,1,0:T(8,128)}) %tuple.56, (s32[]{:T(128)}, s32[512]{0:T(512)S(1)}, s32[]{:T(128)}, ...), branch_computations={%region_1.0_spmd, %region_2.4_spmd} | conditional | flops 1102328832 | bytes 48771228 | solution.py:68
  231.8 4.0 %bitcast_add_fusion = f32[1,8,512,128]{3,2,1,0:T(8,128)S(1)} fusion(f32[1,8,512,128]{3,2,1,0:T(8,128)S(1)} %copy-done.2, f32[512,512,8]{1,0,2:T(8,128)S(1)} %get-tuple-element.274, f32[8,512]{1,0:T(8,128)S(1)} %bitcast.145, pred[512,512]{0,1:T(8,128)(4,1)S(1)} %broadcast_compare_fusion, f32[8,512]{1,0:T(8,128)S(1)} %get-tuple-element.271, ...), kind=kOutput, calls=%fused_computation.11 | convolution fusion | flops 548405248 | bytes 13008904 | tf_op jit(solution)/shard_map/while/body/eval_jaxpr/cond/branch_1_fun/hgtk,khd->hgtd/dot_general | solution.py:50
  238.0 9.0 %conditional.3 = ((f32[1,8,512]{2,1,0:T(8,128)S(1)}, f32[1,8,512]{2,1,0:T(8,128)S(1)}, f32[1,8,512,128]{3,2,1,0:T(8,128)})) conditional(s32[]{:T(128)} %convert_element_type.97, (f32[1,8,512]{2,1,0:T(8,128)S(1)}, f32[1,8,512]{2,1,0:T(8,128)S(1)}, f32[1,8,512,128]{3,2,1,0:T(8,128)}) %tuple.56, (s32[]{:T(128)}, s32[512]{0:T(512)S(1)}, s32[]{:T(128)}, ...), branch_computations={%region_1.0_spmd, %region_2.4_spmd} | conditional | flops 1102328832 | bytes 48771228 | solution.py:68
  240.8 4.0 %bitcast_add_fusion = f32[1,8,512,128]{3,2,1,0:T(8,128)S(1)} fusion(f32[1,8,512,128]{3,2,1,0:T(8,128)S(1)} %copy-done.2, f32[512,512,8]{1,0,2:T(8,128)S(1)} %get-tuple-element.274, f32[8,512]{1,0:T(8,128)S(1)} %bitcast.145, pred[512,512]{0,1:T(8,128)(4,1)S(1)} %broadcast_compare_fusion, f32[8,512]{1,0:T(8,128)S(1)} %get-tuple-element.271, ...), kind=kOutput, calls=%fused_computation.11 | convolution fusion | flops 548405248 | bytes 13008904 | tf_op jit(solution)/shard_map/while/body/eval_jaxpr/cond/branch_1_fun/hgtk,khd->hgtd/dot_general | solution.py:50
  247.0 9.0 %conditional.3 = ((f32[1,8,512]{2,1,0:T(8,128)S(1)}, f32[1,8,512]{2,1,0:T(8,128)S(1)}, f32[1,8,512,128]{3,2,1,0:T(8,128)})) conditional(s32[]{:T(128)} %convert_element_type.97, (f32[1,8,512]{2,1,0:T(8,128)S(1)}, f32[1,8,512]{2,1,0:T(8,128)S(1)}, f32[1,8,512,128]{3,2,1,0:T(8,128)}) %tuple.56, (s32[]{:T(128)}, s32[512]{0:T(512)S(1)}, s32[]{:T(128)}, ...), branch_computations={%region_1.0_spmd, %region_2.4_spmd} | conditional | flops 1102328832 | bytes 48771228 | solution.py:68
  247.2 2.5 fusion.2
  249.8 4.0 %bitcast_add_fusion = f32[1,8,512,128]{3,2,1,0:T(8,128)S(1)} fusion(f32[1,8,512,128]{3,2,1,0:T(8,128)S(1)} %copy-done.2, f32[512,512,8]{1,0,2:T(8,128)S(1)} %get-tuple-element.274, f32[8,512]{1,0:T(8,128)S(1)} %bitcast.145, pred[512,512]{0,1:T(8,128)(4,1)S(1)} %broadcast_compare_fusion, f32[8,512]{1,0:T(8,128)S(1)} %get-tuple-element.271, ...), kind=kOutput, calls=%fused_computation.11 | convolution fusion | flops 548405248 | bytes 13008904 | tf_op jit(solution)/shard_map/while/body/eval_jaxpr/cond/branch_1_fun/hgtk,khd->hgtd/dot_general | solution.py:50
  256.0 9.0 %conditional.3 = ((f32[1,8,512]{2,1,0:T(8,128)S(1)}, f32[1,8,512]{2,1,0:T(8,128)S(1)}, f32[1,8,512,128]{3,2,1,0:T(8,128)})) conditional(s32[]{:T(128)} %convert_element_type.97, (f32[1,8,512]{2,1,0:T(8,128)S(1)}, f32[1,8,512]{2,1,0:T(8,128)S(1)}, f32[1,8,512,128]{3,2,1,0:T(8,128)}) %tuple.56, (s32[]{:T(128)}, s32[512]{0:T(512)S(1)}, s32[]{:T(128)}, ...), branch_computations={%region_1.0_spmd, %region_2.4_spmd} | conditional | flops 1102328832 | bytes 48771228 | solution.py:68
  258.8 4.0 %bitcast_add_fusion = f32[1,8,512,128]{3,2,1,0:T(8,128)S(1)} fusion(f32[1,8,512,128]{3,2,1,0:T(8,128)S(1)} %copy-done.2, f32[512,512,8]{1,0,2:T(8,128)S(1)} %get-tuple-element.274, f32[8,512]{1,0:T(8,128)S(1)} %bitcast.145, pred[512,512]{0,1:T(8,128)(4,1)S(1)} %broadcast_compare_fusion, f32[8,512]{1,0:T(8,128)S(1)} %get-tuple-element.271, ...), kind=kOutput, calls=%fused_computation.11 | convolution fusion | flops 548405248 | bytes 13008904 | tf_op jit(solution)/shard_map/while/body/eval_jaxpr/cond/branch_1_fun/hgtk,khd->hgtd/dot_general | solution.py:50
  (244 shorter events, 82.5 us)
Async XLA Ops:
  7.2 3.2 %copy-start = (bf16[8192,128]{1,0:T(8,128)(2,1)S(1)}, bf16[8192,128]{1,0:T(8,128)(2,1)}, u32[]{:S(2)}) copy-start(bf16[8192,128]{1,0:T(8,128)(2,1)} %param.15) | copy-start | bytes 6291460
  7.2 112.2 %all-gather.2.cloned.1.call-start = ((), (), s32[]{:S(2)}) async-start(), calls=%async_computation.1 | async-start | bytes 4456448 | tf_op jit(solution)/shard_map/all_gather | solution.py:58
  7.2 9.6 %copy-start.4 = (bf16[8192,128]{1,0:T(8,128)(2,1)S(1)}, bf16[8192,128]{1,0:T(8,128)(2,1)}, u32[]{:S(2)}) copy-start(bf16[8192,128]{1,0:T(8,128)(2,1)} %param.16) | copy-start | bytes 6291460
  7.2 9.6 %copy-start.9 = (bf16[512,8192]{1,0:T(8,128)(2,1)S(1)}, bf16[512,8192]{1,0:T(8,128)(2,1)}, u32[]{:S(2)}) copy-start(bf16[512,8192]{1,0:T(8,128)(2,1)} %param.13) | copy-start | bytes 25165828
  16.8 12.0 %copy-start.6 = (s32[8,16]{1,0:T(8,128)S(1)}, s32[8,16]{1,0:T(8,128)}, u32[]{:S(2)}) copy-start(s32[8,16]{1,0:T(8,128)} %param.20) | copy-start | bytes 1540
  16.8 12.1 %copy-start.10 = (s32[1,32]{1,0:T(1,128)S(1)}, s32[1,32]{1,0:T(1,128)}, u32[]{:S(2)}) copy-start(s32[1,32]{1,0:T(1,128)} %param.21) | copy-start | bytes 388
  16.8 12.6 %copy-start.8 = (s32[8]{0:T(128)S(1)}, s32[8]{0:T(128)}, u32[]{:S(2)}) copy-start(s32[8]{0:T(128)} %param.19) | copy-start | bytes 100
  16.8 12.7 %copy-start.5 = (bf16[4,8,1024]{2,1,0:T(8,128)(2,1)S(1)}, bf16[4,8,1024]{2,1,0:T(8,128)(2,1)}, u32[]{:S(2)}) copy-start(bf16[4,8,1024]{2,1,0:T(8,128)(2,1)} %param.17) | copy-start | bytes 196612
  21.7 48.3 %all-to-all-start = ((bf16[32,16,2,128]{3,2,1,0:T(2,128)(2,1)}), bf16[32,16,2,128]{3,2,1,0:T(2,128)(2,1)S(1)}, u32[]{:S(2)}, u32[]{:S(2)}) async-start(bf16[32,16,2,128]{3,2,1,0:T(2,128)(2,1)} %pad_maximum_fusion.1), calls=%async_computation | async-start | bytes 524288 | tf_op jit(solution)/shard_map/all_to_all | solution.py:82
  28.9 24.8 %copy-start.7 = (pred[4,4]{1,0:T(4,128)(4,1)}, pred[4,4]{1,0:T(4,128)(4,1)S(1)}, u32[]{:S(2)}) copy-start(pred[4,4]{1,0:T(4,128)(4,1)S(1)} %iota_compare_fusion.1) | copy-start | bytes 52
  44.0 9.7 %copy-start.1 = (bf16[4,8,8192]{2,1,0:T(8,128)(2,1)}, bf16[4,8,8192]{2,1,0:T(8,128)(2,1)S(1)}, u32[]{:S(2)}) copy-start(bf16[4,8,8192]{2,1,0:T(8,128)(2,1)S(1)} %all_gather.7) | copy-start | bytes 1572868
  44.0 10.8 %slice-start = ((s8[8388608]{0:T(1024)(128)(4,1)}), s8[4194304]{0:T(1024)(128)(4,1)S(1)}, s32[]{:S(2)}) async-start(s8[8388608]{0:T(1024)(128)(4,1)} %bitcast.157), calls=%async_computation.2 | async-start | bytes 8388608
  44.5 10.3 %slice-start.1 = ((s8[8388608]{0:T(1024)(128)(4,1)}), s8[4194304]{0:T(1024)(128)(4,1)S(1)}, s32[]{:S(2)}) async-start(s8[8388608]{0:T(1024)(128)(4,1)} %bitcast.157), calls=%async_computation.3 | async-start | bytes 8388608
  120.9 2.8 %copy-start.2 = (f32[1,8,512,128]{3,2,1,0:T(8,128)S(1)}, f32[1,8,512,128]{3,2,1,0:T(8,128)}, u32[]{:S(2)}) copy-start(f32[1,8,512,128]{3,2,1,0:T(8,128)} %get-tuple-element.201) | copy-start | bytes 6291460 | tf_op jit(solution)/shard_map/while/body/eval_jaxpr/cond
  127.7 2.1 copy-start.3
  129.9 2.8 %copy-start.2 = (f32[1,8,512,128]{3,2,1,0:T(8,128)S(1)}, f32[1,8,512,128]{3,2,1,0:T(8,128)}, u32[]{:S(2)}) copy-start(f32[1,8,512,128]{3,2,1,0:T(8,128)} %get-tuple-element.201) | copy-start | bytes 6291460 | tf_op jit(solution)/shard_map/while/body/eval_jaxpr/cond
  136.7 2.1 copy-start.3
  138.9 2.8 %copy-start.2 = (f32[1,8,512,128]{3,2,1,0:T(8,128)S(1)}, f32[1,8,512,128]{3,2,1,0:T(8,128)}, u32[]{:S(2)}) copy-start(f32[1,8,512,128]{3,2,1,0:T(8,128)} %get-tuple-element.201) | copy-start | bytes 6291460 | tf_op jit(solution)/shard_map/while/body/eval_jaxpr/cond
  145.7 2.1 copy-start.3
  147.9 2.8 %copy-start.2 = (f32[1,8,512,128]{3,2,1,0:T(8,128)S(1)}, f32[1,8,512,128]{3,2,1,0:T(8,128)}, u32[]{:S(2)}) copy-start(f32[1,8,512,128]{3,2,1,0:T(8,128)} %get-tuple-element.201) | copy-start | bytes 6291460 | tf_op jit(solution)/shard_map/while/body/eval_jaxpr/cond
  154.7 2.1 copy-start.3
  156.9 2.8 %copy-start.2 = (f32[1,8,512,128]{3,2,1,0:T(8,128)S(1)}, f32[1,8,512,128]{3,2,1,0:T(8,128)}, u32[]{:S(2)}) copy-start(f32[1,8,512,128]{3,2,1,0:T(8,128)} %get-tuple-element.201) | copy-start | bytes 6291460 | tf_op jit(solution)/shard_map/while/body/eval_jaxpr/cond
  163.7 2.1 copy-start.3
  165.9 2.8 %copy-start.2 = (f32[1,8,512,128]{3,2,1,0:T(8,128)S(1)}, f32[1,8,512,128]{3,2,1,0:T(8,128)}, u32[]{:S(2)}) copy-start(f32[1,8,512,128]{3,2,1,0:T(8,128)} %get-tuple-element.201) | copy-start | bytes 6291460 | tf_op jit(solution)/shard_map/while/body/eval_jaxpr/cond
  172.7 2.1 copy-start.3
  174.9 2.8 %copy-start.2 = (f32[1,8,512,128]{3,2,1,0:T(8,128)S(1)}, f32[1,8,512,128]{3,2,1,0:T(8,128)}, u32[]{:S(2)}) copy-start(f32[1,8,512,128]{3,2,1,0:T(8,128)} %get-tuple-element.201) | copy-start | bytes 6291460 | tf_op jit(solution)/shard_map/while/body/eval_jaxpr/cond
  181.8 2.1 copy-start.3
  183.9 2.8 %copy-start.2 = (f32[1,8,512,128]{3,2,1,0:T(8,128)S(1)}, f32[1,8,512,128]{3,2,1,0:T(8,128)}, u32[]{:S(2)}) copy-start(f32[1,8,512,128]{3,2,1,0:T(8,128)} %get-tuple-element.201) | copy-start | bytes 6291460 | tf_op jit(solution)/shard_map/while/body/eval_jaxpr/cond
  190.8 2.1 copy-start.3
  192.9 2.8 %copy-start.2 = (f32[1,8,512,128]{3,2,1,0:T(8,128)S(1)}, f32[1,8,512,128]{3,2,1,0:T(8,128)}, u32[]{:S(2)}) copy-start(f32[1,8,512,128]{3,2,1,0:T(8,128)} %get-tuple-element.201) | copy-start | bytes 6291460 | tf_op jit(solution)/shard_map/while/body/eval_jaxpr/cond
  199.8 2.1 copy-start.3
  201.9 2.8 %copy-start.2 = (f32[1,8,512,128]{3,2,1,0:T(8,128)S(1)}, f32[1,8,512,128]{3,2,1,0:T(8,128)}, u32[]{:S(2)}) copy-start(f32[1,8,512,128]{3,2,1,0:T(8,128)} %get-tuple-element.201) | copy-start | bytes 6291460 | tf_op jit(solution)/shard_map/while/body/eval_jaxpr/cond
  208.8 2.1 copy-start.3
  210.9 2.8 %copy-start.2 = (f32[1,8,512,128]{3,2,1,0:T(8,128)S(1)}, f32[1,8,512,128]{3,2,1,0:T(8,128)}, u32[]{:S(2)}) copy-start(f32[1,8,512,128]{3,2,1,0:T(8,128)} %get-tuple-element.201) | copy-start | bytes 6291460 | tf_op jit(solution)/shard_map/while/body/eval_jaxpr/cond
  217.8 2.1 copy-start.3
  220.0 2.8 %copy-start.2 = (f32[1,8,512,128]{3,2,1,0:T(8,128)S(1)}, f32[1,8,512,128]{3,2,1,0:T(8,128)}, u32[]{:S(2)}) copy-start(f32[1,8,512,128]{3,2,1,0:T(8,128)} %get-tuple-element.201) | copy-start | bytes 6291460 | tf_op jit(solution)/shard_map/while/body/eval_jaxpr/cond
  226.8 2.1 copy-start.3
  229.0 2.8 %copy-start.2 = (f32[1,8,512,128]{3,2,1,0:T(8,128)S(1)}, f32[1,8,512,128]{3,2,1,0:T(8,128)}, u32[]{:S(2)}) copy-start(f32[1,8,512,128]{3,2,1,0:T(8,128)} %get-tuple-element.201) | copy-start | bytes 6291460 | tf_op jit(solution)/shard_map/while/body/eval_jaxpr/cond
  235.8 2.1 copy-start.3
  238.0 2.8 %copy-start.2 = (f32[1,8,512,128]{3,2,1,0:T(8,128)S(1)}, f32[1,8,512,128]{3,2,1,0:T(8,128)}, u32[]{:S(2)}) copy-start(f32[1,8,512,128]{3,2,1,0:T(8,128)} %get-tuple-element.201) | copy-start | bytes 6291460 | tf_op jit(solution)/shard_map/while/body/eval_jaxpr/cond
  244.8 2.1 copy-start.3
  247.0 2.8 %copy-start.2 = (f32[1,8,512,128]{3,2,1,0:T(8,128)S(1)}, f32[1,8,512,128]{3,2,1,0:T(8,128)}, u32[]{:S(2)}) copy-start(f32[1,8,512,128]{3,2,1,0:T(8,128)} %get-tuple-element.201) | copy-start | bytes 6291460 | tf_op jit(solution)/shard_map/while/body/eval_jaxpr/cond
  253.8 2.1 copy-start.3
  256.0 2.8 %copy-start.2 = (f32[1,8,512,128]{3,2,1,0:T(8,128)S(1)}, f32[1,8,512,128]{3,2,1,0:T(8,128)}, u32[]{:S(2)}) copy-start(f32[1,8,512,128]{3,2,1,0:T(8,128)} %get-tuple-element.201) | copy-start | bytes 6291460 | tf_op jit(solution)/shard_map/while/body/eval_jaxpr/cond
  262.9 2.1 copy-start.3
Sparse Core Ops, SparseCore 0:
  20.1 99.2 all-gather.1
where the time goes:
time: 277 us; the launch traced here: 276 us
  matrix products  141 us (51%)
  other arithmetic  42.9 us (15%)
  waiting for transfers between devices  34.8 us (13%)
  local copies, waits for them, and re-layouts  18.9 us (7%)
  blocking collectives  14.5 us (5%)
  between operations  14.3 us (5%)
  starting transfers between devices  7.12 us (3%)
    dot_general x16, matrix products, absorb(): jnp.einsum('hgtk,khd->hgtd', weights.astype(jnp.bfloat16), block_values,...  64.4 us
    dot_general x16, matrix products, absorb(): jnp.einsum('thgd,khd->hgtk', queries, block_keys, preferred_element_type=...  40.5 us
    all_gather x1, waiting for transfers between devices, per_device(): kv_piece = lax.all_gather(packed, ('seq', 'pool'), axis=0, tiled=True)  34.8 us
    reduce_sum x16, other arithmetic, absorb(): totals = totals * rescale + jnp.sum(weights, axis=-1)  32.5 us
    all_gather x1, blocking collectives, per_device(): step_x = lax.all_gather(dec_x, 'tensor', axis=2, tiled=True)  14.5 us
    dot_general x1, matrix products, per_device(): jnp.dot(pre_x, w_query, preferred_element_type=jnp.float32)  12.5 us
    dot_general x1, matrix products, per_device(): jnp.dot(flat_x, w_query, preferred_element_type=jnp.float32)  9.24 us
    all_to_all x1, starting transfers between devices, per_device(): lax.all_to_all(page_blocks, ('seq', 'pool'), split_axis=0, concat_axis=0,...  7.09 us
  transfers between devices with their start and end apart: 2, of which 1 were waited for; matrix products, arithmetic and copies ran while one was open for 16% of the time, Pallas kernels for 0%

commit v1 on v0

v1 whole, which is shorter than its diff:
```python
import functools

import jax
import jax.numpy as jnp
from jax import lax
from jax.experimental import pallas as pl
from jax.experimental.pallas import tpu as pltpu
from jax.sharding import PartitionSpec as P

MESH = pl.DeviceIdType.MESH
BF16 = jnp.bfloat16
F32 = jnp.float32

D = 8192
HD = 128
HEADS = 8
TOK = 512
GROUPS = 16
PAGE = 16
MAXP = 16
PAGES = 128
ROWS = 8
STEPS = 4
DEC = ROWS * STEPS
ALL = TOK + DEC
TILE_TOK = 64
TILES = TOK // TILE_TOK
TILE = TILE_TOK * HEADS
CACHE_ROWS = PAGES * PAGE * 2
NEW_ROWS = 512
SCALE = HD ** (-0.5) * 1.4426950408889634
LOW = -1e30
XC = 8
QK = 4
QN = 2
LENT = 4
TAKES = (4, 3, 3, 3, 2, 2, 1, 0)
JOIN = 3
EARLY = 9
TURNS = ((6,), (7, 8), (9, 10), (11,), (12,), (13,), (14,), (15,))

ORDER = (
    (0, 0), (3, 0), (1, 0), (0, 3), (0, 1), (2, 0), (3, 3), (3, 1),
    (1, 3), (1, 1), (2, 3), (2, 1), (0, 2), (3, 2), (1, 2), (2, 2),
)


def sends_after(event):
    near, far = event
    sends = []
    if near == 0 and far == 0:
        sends += [(0, "A+"), (0, "A-"), (1, "A+"), (1, "A-")]
    elif far == 0 and near == 3:
        sends += [(0, "A+")]
    elif far == 0 and near == 1:
        sends += [(1, "A-")]
    if far == 0:
        sends += [(0, "B+"), (0, "B-"), (1, "B+"), (1, "B-")]
    elif far == 3:
        sends += [(0, "B+")]
    elif far == 1:
        sends += [(1, "B-")]
    return sends


def seen_from(event, direction):
    near, far = event
    step = 1 if direction[1] == "+" else -1
    if direction[0] == "A":
        return ((near - step) % 4, far)
    return (near, (far - step) % 4)


SENDS = [(event, half, way) for event in ORDER for half, way in sends_after(event)]


def prefill(
    px, wq, wk, wv, dx,
    pre_out, dq_out, dkv_out, new_out,
    x_s, wkv_s, wq_s, kv_s, kt_s, va_s, of_s, q_s, pacc, acc, m_s, sa_s, sb_s,
    xsem, wksem, wvsem, qsem, dsem_own, dsend, drecv, ssem, rsem, qsend, qrecv, osend, orecv,
):
    seq, tensor, pool = lax.axis_index("seq"), lax.axis_index("tensor"), lax.axis_index("pool")
    x, y, core = seq // 2, pool * 2 + seq % 2, tensor % 2
    g = seq * 2 + pool
    low = g < 8
    other = 15 - g
    last = jnp.where(low, other, g)
    pair = jnp.where(low, g, other)
    count = sum(jnp.where(pair == k, TAKES[k], 0) for k in range(8))
    partner = {"seq": 7 - seq, "pool": 1 - pool}

    def place(near, far):
        ax, ay = (x + near) % 4, (y + far) % 4
        bx, by = (x + far) % 4, (y + near) % 4
        return jnp.where(core == 0, ax, bx), jnp.where(core == 0, ay, by)

    def slot_of(near, far):
        px_, py_ = place(near, far)
        return px_ * 4 + (py_ % 2) * 2 + py_ // 2

    def device(near, far):
        px_, py_ = place(near, far)
        return {"seq": px_ * 2 + py_ % 2, "pool": py_ // 2}

    ways = {"A+": device(1, 0), "A-": device(3, 0), "B+": device(0, 1), "B-": device(0, 3)}

    def x_copy(c):
        cols = pl.ds(pl.multiple_of(c * (D // XC), D // XC), D // XC)
        return pltpu.make_async_copy(px.at[:, cols], x_s.at[pl.ds(0, TOK), cols], xsem.at[c])

    def w_copy(c, ref, at, sem):
        rows = pl.ds(pl.multiple_of(c * (D // XC), D // XC), D // XC)
        return pltpu.make_async_copy(ref.at[rows, :], wkv_s.at[rows, pl.ds(at, HD)], sem.at[c])

    def q_copy(n, k):
        rows = pl.ds(k * (D // QK), D // QK)
        cols = pl.ds(n * (HEADS * HD // QN), HEADS * HD // QN)
        return pltpu.make_async_copy(wq.at[rows, cols], wq_s.at[rows, cols], qsem.at[n * QK + k])

    my_cols = pl.ds(pl.multiple_of(tensor * (D // 8), D // 8), D // 8)
    dec_own = pltpu.make_async_copy(dx, x_s.at[pl.ds(TOK, DEC), my_cols], dsem_own)

    for c in range(XC):
        x_copy(c).start()
        w_copy(c, wk, 0, wksem).start()
        w_copy(c, wv, HD, wvsem).start()
    dec_own.start()
    for n in range(QN):
        for k in range(QK):
            q_copy(n, k).start()

    barrier = pltpu.get_barrier_semaphore()
    for way in ways.values():
        pl.semaphore_signal(barrier, inc=1, device_id=way, device_id_type=MESH)
    pl.semaphore_signal(barrier, inc=1, device_id=partner, device_id_type=MESH)
    for k in range(1, 8):
        pl.semaphore_signal(
            barrier, inc=1, device_id={"tensor": (tensor + k) % 8}, device_id_type=MESH
        )
    pl.semaphore_wait(barrier, 12)

    def dec_copy(k):
        return pltpu.make_async_remote_copy(
            src_ref=dx,
            dst_ref=x_s.at[pl.ds(TOK, DEC), my_cols],
            send_sem=dsend.at[k - 1],
            recv_sem=drecv.at[k - 1],
            device_id={"tensor": (tensor + k) % 8},
            device_id_type=MESH,
        )

    def dec_arrival(k):
        cols = pl.ds(pl.multiple_of(((tensor + 8 - k) % 8) * (D // 8), D // 8), D // 8)
        return pltpu.make_async_remote_copy(
            src_ref=dx,
            dst_ref=x_s.at[pl.ds(TOK, DEC), cols],
            send_sem=dsend.at[k - 1],
            recv_sem=drecv.at[k - 1],
            device_id={"tensor": (tensor + k) % 8},
            device_id_type=MESH,
        )

    for k in range(1, 8):
        dec_copy(k).start()

    def kv_copy(number):
        event, half, way = SENDS[number]
        slot = slot_of(*event)
        near, far = seen_from(event, way)
        return pltpu.make_async_remote_copy(
            src_ref=kv_s.at[slot, half],
            dst_ref=kv_s.at[slot, half],
            send_sem=ssem.at[number],
            recv_sem=rsem.at[(near * 4 + far) * 2 + half],
            device_id=ways[way],
            device_id_type=MESH,
        )

    def pass_on(event):
        for number, (of, _, _) in enumerate(SENDS):
            if of == event:
                kv_copy(number).start()

    def arrive(event):
        near, far = event
        slot = slot_of(near, far)
        for half in range(2):
            pltpu.make_async_remote_copy(
                src_ref=kv_s.at[slot, half],
                dst_ref=kv_s.at[slot, half],
                send_sem=ssem.at[0],
                recv_sem=rsem.at[(near * 4 + far) * 2 + half],
                device_id=ways["A+"],
                device_id_type=MESH,
            ).wait_recv()
        pass_on(event)

    def lend(t, n):
        rows = pl.ds(n * (TILE // QN), TILE // QN)
        return pltpu.make_async_remote_copy(
            src_ref=q_s.at[TILES - LENT + t, rows],
            dst_ref=q_s.at[TILES + t + count - LENT, rows],
            send_sem=qsend.at[t * QN + n],
            recv_sem=qrecv.at[t * QN + n],
            device_id=partner,
            device_id_type=MESH,
        )

    def give_back(f):
        at = pl.ds(pl.multiple_of((TILES - count + f) * TILE_TOK, TILE_TOK), TILE_TOK)
        return pltpu.make_async_remote_copy(
            src_ref=of_s.at[f],
            dst_ref=pre_out.at[at, :],
            send_sem=osend.at[f],
            recv_sem=orecv.at[f],
            device_id=partner,
            device_id_type=MESH,
        )

    def lent(t):
        return count >= LENT - t

    def clear(j, carry):
        acc[j] = jnp.zeros((TILE, 2 * HD), F32)
        m_s[j] = jnp.full((TILE, HD), LOW, F32)
        return carry

    def fill(i, carry):
        va_s[i, :, HD:] = jnp.ones((TOK, HD), BF16)
        return carry

    lax.fori_loop(0, TILES + LENT, clear, 0)
    lax.fori_loop(0, GROUPS, fill, 0)

    def kv_step(c, carry):
        x_copy(c).wait()
        w_copy(c, wk, 0, wksem).wait()
        w_copy(c, wv, HD, wvsem).wait()
        at = pl.ds(pl.multiple_of(c * (D // XC), D // XC), D // XC)
        part = jnp.dot(x_s[0:TOK, at], wkv_s[at, :], preferred_element_type=F32)

        @pl.when(c == 0)
        def _():
            pacc[0:TOK, 0:256] = part

        @pl.when(c > 0)
        def _():
            pacc[0:TOK, 0:256] += part

        return carry

    lax.fori_loop(0, XC, kv_step, 0)
    kv_s[g, 0] = pacc[0:TOK, 0:HD].astype(BF16)
    kv_s[g, 1] = pacc[0:TOK, HD : 2 * HD].astype(BF16)
    pass_on(ORDER[0])

    dec_own.wait()
    for k in range(1, 8):
        dec_arrival(k).wait_recv()

    width = HEADS * HD // QN
    for n in range(QN):
        for k in range(QK):
            q_copy(n, k).wait()
            at = slice(k * (D // QK), (k + 1) * (D // QK))
            part = jnp.dot(
                x_s[:, at], wq_s[at, n * width : (n + 1) * width], preferred_element_type=F32
            )
            if k == 0:
                pacc[...] = part
            else:
                pacc[...] += part
        for hh in range(HEADS // QN):
            h = n * (HEADS // QN) + hh
            for j in range(TILES):
                q_s[j, h * TILE_TOK : (h + 1) * TILE_TOK, :] = (
                    pacc[j * TILE_TOK : (j + 1) * TILE_TOK, hh * HD : (hh + 1) * HD] * SCALE
                ).astype(BF16)
            dq_out[h * DEC : (h + 1) * DEC, :] = (
                pacc[TOK:ALL, hh * HD : (hh + 1) * HD] * SCALE
            ).astype(BF16)
        for t in range(LENT):

            @pl.when(jnp.logical_not(low) & lent(t))
            def _():
                lend(t, n).start()

        if n == 0:
            arrive(ORDER[1])
            arrive(ORDER[2])
    dkv = jnp.dot(x_s[TOK:ALL, :], wkv_s[...], preferred_element_type=F32)
    dkv_out[0] = dkv[:, 0:HD].astype(BF16)
    dkv_out[1] = dkv[:, HD : 2 * HD].astype(BF16)

    for event in ORDER[3:6]:
        arrive(event)

    def prepare(i, slot):
        kt_s[i] = kv_s[slot, 0].T
        va_s[i, :, 0:HD] = kv_s[slot, 1]

    def score(item, buf):
        j, i = item
        buf[...] = jnp.dot(q_s[j], kt_s[i], preferred_element_type=F32)

    def absorb(item, buf, masked):
        j, i = item
        cuts = [buf[:, k * HD : (k + 1) * HD] for k in range(TOK // HD)]
        if masked:
            first = jnp.where(j < TILES, j, j - count) * TILE_TOK
            row = (lax.broadcasted_iota(jnp.int32, (TILE, HD), 0) & (TILE_TOK - 1)) + first
            ahead = lax.broadcasted_iota(jnp.int32, (TILE, HD), 1) - row
            cuts = [jnp.where(ahead <= -k * HD, c, LOW) for k, c in enumerate(cuts)]
        old = m_s[j]
        best = functools.reduce(jnp.maximum, cuts)
        top = jnp.maximum(
            old, jnp.broadcast_to(jnp.max(best, axis=1, keepdims=True), (TILE, HD))
        )
        p = jnp.concatenate([jnp.exp2(c - top).astype(BF16) for c in cuts], axis=1)
        o = jnp.dot(p, va_s[i], preferred_element_type=F32)
        shrink = jnp.exp2(old - top)
        acc[j] = acc[j] * jnp.concatenate([shrink, shrink], axis=1) + o
        m_s[j] = top

    def run(n, item, masked):
        @pl.when(n > 0)
        def _():
            score(item(0), sa_s)

        def two(t, carry):
            score(item(2 * t + 1), sb_s)
            absorb(item(2 * t), sa_s, masked)
            score(item(jnp.minimum(2 * t + 2, n - 1)), sa_s)
            absorb(item(2 * t + 1), sb_s, masked)
            return carry

        lax.fori_loop(0, n // 2, two, 0)

        @pl.when(n % 2 == 1)
        def _():
            absorb(item(n - 1), sa_s, masked)

    own = jnp.where(low, TILES, TILES - count)
    every = jnp.where(low, TILES + count, own)

    prepare(0, g)
    run(own, lambda t: (t, 0), True)

    def slot_at(i):
        near = sum(jnp.where(i == e, ORDER[e][0], 0) for e in range(16))
        far = sum(jnp.where(i == e, ORDER[e][1], 0) for e in range(16))
        return slot_of(near, far)

    def block(i, carry):
        for turn, events in enumerate(TURNS):

            @pl.when(i == turn + 1)
            def _():
                for e in events:
                    arrive(ORDER[e])

        @pl.when(i == JOIN)
        def _():
            for t in range(LENT):
                for n in range(QN):

                    @pl.when(low & lent(t))
                    def _():
                        lend(t, n).wait_recv()

        slot = slot_at(i)
        joined = (i >= JOIN) & (i <= EARLY)

        @pl.when(slot <= last)
        def _():
            prepare(i, slot)

        start = jnp.where(slot < g, 0, TILES)
        stop = jnp.where(joined, every, own)
        n = jnp.where(slot < last, jnp.maximum(stop - start, 0), 0)
        run(n, lambda t: (start + t, i), False)

        @pl.when(joined & (slot == last))
        def _():
            run(every - TILES, lambda t: (TILES + t, i), True)

        return carry

    lax.fori_loop(1, EARLY + 1, block, 0)

    def prepare_late(i, carry):
        slot = slot_at(i)

        @pl.when(slot <= last)
        def _():
            prepare(i, slot)

        return carry

    lax.fori_loop(EARLY + 1, 16, prepare_late, 0)

    def finish(j, h):
        rows = slice(h * TILE_TOK, (h + 1) * TILE_TOK)
        return (acc[j, rows, 0:HD] / acc[j, rows, HD:]).astype(BF16)

    due = [e for e in range(16) if e < JOIN or e > EARLY]
    wanted = [jnp.where(slot_of(*ORDER[e]) < last, 1, 0) for e in due]
    before = [sum(wanted[:k], jnp.int32(0)) for k in range(len(due))]

    def due_at(t):
        return sum(
            jnp.where((wanted[k] == 1) & (before[k] == t), due[k], 0) for k in range(len(due))
        )

    def late(j, carry):
        run(before[-1] + wanted[-1], lambda t: (j, due_at(t)), False)
        for h in range(HEADS):
            of_s[j - TILES, :, h * HD : (h + 1) * HD] = finish(j, h)
        for f in range(LENT):

            @pl.when(j == TILES + f)
            def _():
                give_back(f).start()

        return carry

    lax.fori_loop(TILES, every, late, 0)

    def late_own(i, carry):
        run(jnp.where(slot_at(i) < g, own, 0), lambda t: (t, i), False)
        return carry

    lax.fori_loop(EARLY + 1, 16, late_own, 0)

    for j in range(TILES):

        @pl.when(j < own)
        def _():
            for h in range(HEADS):
                pre_out[j * TILE_TOK : (j + 1) * TILE_TOK, h * HD : (h + 1) * HD] = finish(j, h)

    mine = NEW_ROWS // GROUPS
    at = pl.ds(pl.multiple_of(g * mine, mine), mine)
    for src in range(GROUPS):
        for half in range(2):
            new_out[half, src * mine : (src + 1) * mine, :] = kv_s[src, half, at, :]

    for t in range(LENT):

        @pl.when((t < count) & low)
        def _():
            give_back(t).wait_send()

        @pl.when(lent(t) & jnp.logical_not(low))
        def _():
            for n in range(QN):
                lend(t, n).wait_send()

        @pl.when((t < count) & jnp.logical_not(low))
        def _():
            give_back(t).wait_recv()

    for k in range(1, 8):
        dec_copy(k).wait_send()
    for number in range(len(SENDS)):
        kv_copy(number).wait_send()


def decode(
    table, lens, dest, pre_in, cache, dq, dkv, new,
    pre_out, dec_out,
    cf_s, sd_s, sem,
):
    hand_on = pltpu.make_async_copy(pre_in, pre_out, sem)
    hand_on.start()
    cf_s[...] = cache[...].astype(F32)
    tokens = PAGES * PAGE

    lane = lax.broadcasted_iota(jnp.int32, (1, PAGES), 1)
    limits = []
    for r in range(ROWS):
        limit = jnp.zeros((1, PAGES), jnp.int32)
        for j in range(MAXP):
            left = jnp.clip(lens[r] - j * PAGE, 0, PAGE)
            limit = jnp.where(lane == table[r, j], left, limit)
        limits.append(limit)
    limit = jnp.concatenate(limits, axis=0).astype(F32)
    new_page = lax.broadcasted_iota(jnp.int32, (1, NEW_ROWS), 1) >> 4
    new_slot = jnp.zeros((1, NEW_ROWS), jnp.int32)
    replaced = jnp.zeros((1, PAGES), jnp.int32)
    for m in range(TOK // PAGE):
        new_slot = jnp.where(new_page == m, dest[0, m], new_slot)
        replaced = jnp.where(lane == dest[0, m], 1, replaced)
    old_limit = jnp.where(replaced == 1, 0.0, limit).astype(BF16)

    def bias(limit, page):
        total = page.shape[1]
        pick = jnp.where(
            lax.broadcasted_iota(jnp.int32, (PAGES, total), 0) == page, 1.0, 0.0
        ).astype(BF16)
        held = jnp.dot(limit, pick, preferred_element_type=F32)
        offset = lax.broadcasted_iota(jnp.int32, (1, total), 1) & (PAGE - 1)
        return jnp.where(offset.astype(F32) < held, 0.0, LOW)

    def scores(keys):
        return lax.dot_general(
            dq[...], keys, (((1,), (1,)), ((), ())), preferred_element_type=F32
        )

    def over_queries(mask):
        return jnp.broadcast_to(mask[None], (HEADS * STEPS, *mask.shape)).reshape(
            HEADS * DEC, mask.shape[1]
        )

    query_row = lax.broadcasted_iota(jnp.int32, (HEADS * DEC, DEC), 0)
    key_row = lax.broadcasted_iota(jnp.int32, (HEADS * DEC, DEC), 1)
    tok_ok = ((query_row & (ROWS - 1)) == (key_row & (ROWS - 1))) & (
        (key_row >> 3) <= ((query_row & (DEC - 1)) >> 3)
    )
    part = 512
    parts = tokens // part
    s_tok = jnp.where(tok_ok, scores(dkv[0]), LOW)
    top = jnp.max(s_tok, axis=1, keepdims=True)
    s_new = scores(new[0]) + over_queries(bias(limit.astype(BF16), new_slot))
    top = jnp.maximum(top, jnp.max(s_new, axis=1, keepdims=True))
    for i in range(parts):
        cols = slice(i * part, (i + 1) * part)
        page = (lax.broadcasted_iota(jnp.int32, (1, part), 1) >> 4) + i * (part // PAGE)
        keys = cf_s[pl.ds(2 * i * part, part, stride=2), :].astype(BF16)
        s_old = scores(keys) + over_queries(bias(old_limit, page))
        sd_s[:, cols] = s_old
        top = jnp.maximum(top, jnp.max(s_old, axis=1, keepdims=True))
    p = jnp.exp2(s_tok - top)
    total = jnp.sum(p, axis=1, keepdims=True)
    mixed = jnp.dot(p.astype(BF16), dkv[1], preferred_element_type=F32)
    p = jnp.exp2(s_new - top)
    total = total + jnp.sum(p, axis=1, keepdims=True)
    mixed = mixed + jnp.dot(p.astype(BF16), new[1], preferred_element_type=F32)
    for i in range(parts):
        p = jnp.exp2(sd_s[:, i * part : (i + 1) * part] - top)
        total = total + jnp.sum(p, axis=1, keepdims=True)
        values = cf_s[pl.ds(2 * i * part + 1, part, stride=2), :].astype(BF16)
        mixed = mixed + jnp.dot(p.astype(BF16), values, preferred_element_type=F32)
    mixed = mixed / total
    for h in range(HEADS):
        dec_out[:, h * HD : (h + 1) * HD] = mixed[h * DEC : (h + 1) * DEC, :].astype(BF16)
    hand_on.wait()


def per_device(pre_x, w_query, w_key, w_value, dec_x, cache, lengths, page_table, dest_slots):
    hbm = pl.BlockSpec(memory_space=pltpu.MemorySpace.HBM)
    vmem = pl.BlockSpec(memory_space=pltpu.MemorySpace.VMEM)
    smem = pl.BlockSpec(memory_space=pltpu.MemorySpace.SMEM)
    pre, dq, dkv, new = pl.pallas_call(
        prefill,
        out_shape=(
            jax.ShapeDtypeStruct((TOK, HEADS * HD), BF16),
            jax.ShapeDtypeStruct((HEADS * DEC, HD), BF16),
            jax.ShapeDtypeStruct((2, DEC, HD), BF16),
            jax.ShapeDtypeStruct((2, NEW_ROWS, HD), BF16),
        ),
        in_specs=[hbm] * 5,
        out_specs=(vmem,) * 4,
        scratch_shapes=[
            pltpu.VMEM((ALL, D), BF16),
            pltpu.VMEM((D, 2 * HD), BF16),
            pltpu.VMEM((D, HEADS * HD), BF16),
            pltpu.VMEM((GROUPS, 2, TOK, HD), BF16),
            pltpu.VMEM((GROUPS, HD, TOK), BF16),
            pltpu.VMEM((GROUPS, TOK, 2 * HD), BF16),
            pltpu.VMEM((LENT, TILE_TOK, HEADS * HD), BF16),
            pltpu.VMEM((TILES + LENT, TILE, HD), BF16),
            pltpu.VMEM((ALL, HEADS * HD // QN), F32),
            pltpu.VMEM((TILES + LENT, TILE, 2 * HD), F32),
            pltpu.VMEM((TILES + LENT, TILE, HD), F32),
            pltpu.VMEM((TILE, TOK), F32),
            pltpu.VMEM((TILE, TOK), F32),
            pltpu.SemaphoreType.DMA((XC,)),
            pltpu.SemaphoreType.DMA((XC,)),
            pltpu.SemaphoreType.DMA((XC,)),
            pltpu.SemaphoreType.DMA((QN * QK,)),
            pltpu.SemaphoreType.DMA,
            pltpu.SemaphoreType.DMA((7,)),
            pltpu.SemaphoreType.DMA((7,)),
            pltpu.SemaphoreType.DMA((len(SENDS),)),
            pltpu.SemaphoreType.DMA((32,)),
            pltpu.SemaphoreType.DMA((LENT * QN,)),
            pltpu.SemaphoreType.DMA((LENT * QN,)),
            pltpu.SemaphoreType.DMA((LENT,)),
            pltpu.SemaphoreType.DMA((LENT,)),
        ],
        compiler_params=pltpu.CompilerParams(
            collective_id=0, has_side_effects=True, vmem_limit_bytes=63 * 1024 * 1024
        ),
    )(pre_x, w_query, w_key, w_value, dec_x.reshape(DEC, D // 8))
    pre_out, dec_out = pl.pallas_call(
        decode,
        out_shape=(
            jax.ShapeDtypeStruct((TOK, HEADS * HD), BF16),
            jax.ShapeDtypeStruct((DEC, HEADS * HD), BF16),
        ),
        in_specs=[smem] * 3 + [hbm] + [vmem] * 4,
        out_specs=(hbm, vmem),
        scratch_shapes=[
            pltpu.VMEM((CACHE_ROWS, HD), F32),
            pltpu.VMEM((HEADS * DEC, PAGES * PAGE), F32),
            pltpu.SemaphoreType.DMA,
        ],
        compiler_params=pltpu.CompilerParams(vmem_limit_bytes=63 * 1024 * 1024),
    )(page_table, lengths, dest_slots, pre, cache.reshape(CACHE_ROWS, HD), dq, dkv, new)
    return pre_out, dec_out.reshape(STEPS, ROWS, HEADS * HD)


def solution(mesh):
    in_specs = (
        P(("seq", "pool"), None),
        P(None, "tensor"),
        P(None, "tensor"),
        P(None, "tensor"),
        P(None, ("seq", "pool"), "tensor"),
        P(("seq", "pool"), None, None, "tensor"),
        P(("seq", "pool")),
        P(("seq", "pool"), None),
        P(("seq", "pool"), None),
    )
    out_specs = (P(("seq", "pool"), "tensor"), P(None, ("seq", "pool"), "tensor"))
    return jax.shard_map(
        per_device, mesh=mesh, in_specs=in_specs, out_specs=out_specs, check_vma=False
    )
```

time: 277 us -> 118 us (0.43)
  matrix products: 141 us -> 0 us
  Pallas kernels: 0 us -> 117 us
  other arithmetic: 42.9 us -> 0 us
  waiting for transfers between devices: 34.8 us -> 0 us
  local copies, waits for them, and re-layouts: 18.9 us -> 0 us
  blocking collectives: 14.5 us -> 0 us
  between operations: 14.3 us -> 0.8 us
  starting transfers between devices: 7.12 us -> 0 us
    dot_general x42 -> x0, matrix products: 141 us -> none  [the longest x16 64.4 us: absorb(): jnp.einsum('hgtk,khd->hgtd', weights.astype(jnp.bfloat16), block_values,...]
    pallas_call x0 -> x2, Pallas kernels: none -> 117 us  [the longest x1 82.3 us: per_device(): pl.pallas_call(prefill, out_shape=(jax.ShapeDtypeStruct((TOK, HEADS * HD)...]
    all_gather x1 -> x0, waiting for transfers between devices: 34.8 us -> none  [per_device(): kv_piece = lax.all_gather(packed, ('seq', 'pool'), axis=0, tiled=True)]
    reduce_sum x18 -> x0, other arithmetic: 33.6 us -> none  [the longest x16 32.5 us: absorb(): totals = totals * rescale + jnp.sum(weights, axis=-1)]
    all_gather x1 -> x0, blocking collectives: 14.5 us -> none  [per_device(): step_x = lax.all_gather(dec_x, 'tensor', axis=2, tiled=True)]
    all_to_all x1 -> x0, starting transfers between devices: 7.09 us -> none  [per_device(): lax.all_to_all(page_blocks, ('seq', 'pool'), split_axis=0, concat_axis=0,...]
    gather x2 -> x0, local copies, waits for them, and re-layouts: 6.16 us -> none  [per_device(): context = pool_pages[page_table].reshape(n_rows, -1, 2, kv_local, HD)]
    unnamed x27 -> x0, local copies, waits for them, and re-layouts: 5.44 us -> none
  transfers between devices with their start and end apart: 2 -> 0, of which waited for: 1 -> 0; matrix products, arithmetic and copies ran while one was open for 16% -> 0% of each run, Pallas kernels for 0% -> 0%
where the time goes in v1:
time: 118 us
  Pallas kernels  117 us (99%)
    pallas_call x1, Pallas kernels, per_device(): pl.pallas_call(prefill, out_shape=(jax.ShapeDtypeStruct((TOK, HEADS * HD)...  82.3 us
    pallas_call x1, Pallas kernels, per_device(): pl.pallas_call(decode, out_shape=(jax.ShapeDtypeStruct((TOK, HEADS * HD),...  34.8 us

profile of v1, /device:TPU:30, one launch (start us, length us, event | category | flops | bytes accessed | tf_op | source)
XLA Modules:
  0.0 117.9 jit_solution(10229547555245534239)
XLA Ops:
  0.6 82.3 %shard_map.104 = (bf16[512,1024]{1,0:T(8,128)(2,1)}, bf16[256,128]{1,0:T(8,128)(2,1)}, bf16[2,32,128]{2,1,0:T(8,128)(2,1)}, bf16[2,512,128]{2,1,0:T(8,128)(2,1)}) custom-call(bf16[512,8192]{1,0:T(8,128)(2,1)} %px.1, bf16[8192,1024]{1,0:T(8,128)(2,1)} %wq.1, bf16[8192,128]{1,0:T(8,128)(2,1)} %wk.1, bf16[8192,128]{1,0:T(8,128)(2,1)} %wv.1, ...), custom_call_target="tpu_custom_call" | custom-call | tf_op jit(solution)/shard_map/pallas_call | solution.py:555
  82.9 34.8 %shard_map.105 = (bf16[512,1024]{1,0:T(8,128)(2,1)}, bf16[32,1024]{1,0:T(8,128)(2,1)}) custom-call(s32[8,16]{1,0:T(8,128)} %table.1, s32[8]{0:T(128)} %lens.1, s32[1,32]{1,0:T(1,128)} %dest.1, bf16[512,1024]{1,0:T(8,128)(2,1)} %get-tuple-element.8.pre_in, bf16[4096,128]{1,0:T(8,128)(2,1)} %bitcast.3, bf16[256,128]{1,0:T(8,128)(2,1)} %get-tuple-element.9.dq, ...), custom_call_target="tpu_custom_call" | custom-call | tf_op jit(solution)/shard_map/pallas_call | solution.py:597

commit v2 on v1

--- a/solution.py
+++ b/solution.py
@@ -34,10 +34,10 @@
 QK = 4
 QN = 2
 LENT = 4
-TAKES = (4, 3, 3, 3, 2, 2, 1, 0)
-JOIN = 3
-EARLY = 9
-TURNS = ((6,), (7, 8), (9, 10), (11,), (12,), (13,), (14,), (15,))
+TAKES = (4, 3, 3, 2, 2, 1, 1, 0)
+PAIRS = GROUPS // 2
+CHUNK = 16
+TURNS = ((), (6, 7), (8, 9), (10, 11), (12, 13, 14, 15))
 
 ORDER = (
     (0, 0), (3, 0), (1, 0), (0, 3), (0, 1), (2, 0), (3, 3), (3, 1),
@@ -77,7 +77,7 @@
 def prefill(
     px, wq, wk, wv, dx,
     pre_out, dq_out, dkv_out, new_out,
-    x_s, wkv_s, wq_s, kv_s, kt_s, va_s, of_s, q_s, pacc, acc, m_s, sa_s, sb_s,
+    x_s, wkv_s, wq_s, kv_s, kt_s, va_s, of_s, q_s, pacc, acc, m_s, sa_s, sb_s, pa_s, pb_s,
     xsem, wksem, wvsem, qsem, dsem_own, dsend, drecv, ssem, rsem, qsend, qrecv, osend, orecv,
 ):
     seq, tensor, pool = lax.axis_index("seq"), lax.axis_index("tensor"), lax.axis_index("pool")
@@ -227,11 +227,11 @@
         return carry
 
     def fill(i, carry):
-        va_s[i, :, HD:] = jnp.ones((TOK, HD), BF16)
+        va_s[i, :, HD:] = jnp.ones((2 * TOK, HD), BF16)
         return carry
 
     lax.fori_loop(0, TILES + LENT, clear, 0)
-    lax.fori_loop(0, GROUPS, fill, 0)
+    lax.fori_loop(0, PAIRS, fill, 0)
 
     def kv_step(c, carry):
         x_copy(c).wait()
@@ -296,72 +296,111 @@
     for event in ORDER[3:6]:
         arrive(event)
 
-    def prepare(i, slot):
-        kt_s[i] = kv_s[slot, 0].T
-        va_s[i, :, 0:HD] = kv_s[slot, 1]
+    def prepare(slot):
+        side = pl.ds(pl.multiple_of((slot % 2) * TOK, TOK), TOK)
+        kt_s[slot // 2, :, side] = kv_s[slot, 0].T
+        va_s[slot // 2, side, 0:HD] = kv_s[slot, 1]
+
+    def part_of(item):
+        j, block, whole = item
+        if whole:
+            return j, block, slice(0, 2 * TOK), 2 * TOK
+        return j, block // 2, pl.ds(pl.multiple_of((block % 2) * TOK, TOK), TOK), TOK
 
     def score(item, buf):
-        j, i = item
-        buf[...] = jnp.dot(q_s[j], kt_s[i], preferred_element_type=F32)
-
-    def absorb(item, buf, masked):
-        j, i = item
-        cuts = [buf[:, k * HD : (k + 1) * HD] for k in range(TOK // HD)]
-        if masked:
-            first = jnp.where(j < TILES, j, j - count) * TILE_TOK
-            row = (lax.broadcasted_iota(jnp.int32, (TILE, HD), 0) & (TILE_TOK - 1)) + first
-            ahead = lax.broadcasted_iota(jnp.int32, (TILE, HD), 1) - row
-            cuts = [jnp.where(ahead <= -k * HD, c, LOW) for k, c in enumerate(cuts)]
-        old = m_s[j]
-        best = functools.reduce(jnp.maximum, cuts)
-        top = jnp.maximum(
-            old, jnp.broadcast_to(jnp.max(best, axis=1, keepdims=True), (TILE, HD))
-        )
-        p = jnp.concatenate([jnp.exp2(c - top).astype(BF16) for c in cuts], axis=1)
-        o = jnp.dot(p, va_s[i], preferred_element_type=F32)
-        shrink = jnp.exp2(old - top)
-        acc[j] = acc[j] * jnp.concatenate([shrink, shrink], axis=1) + o
-        m_s[j] = top
-
-    def run(n, item, masked):
+        j, two, side, width = part_of(item)
+        buf[:, 0:width] = jnp.dot(q_s[j], kt_s[two, :, side], preferred_element_type=F32)
+
+    def absorb(item, buf, weights, ahead):
+        j, two, side, width = part_of(item)
+        if ahead is not None:
+            first = jnp.where(j < TILES, j, j - count) * TILE_TOK + ahead
+            lead = lax.broadcasted_iota(jnp.int32, (CHUNK, HD), 1) - lax.broadcasted_iota(
+                jnp.int32, (CHUNK, HD), 0
+            )
+        for c in range(TILE // CHUNK):
+            rows = slice(c * CHUNK, (c + 1) * CHUNK)
+            cuts = [buf[rows, k * HD : (k + 1) * HD] for k in range(width // HD)]
+            if ahead is not None:
+                cuts = [
+                    jnp.where(lead <= first + (c * CHUNK % TILE_TOK - k * HD), cut, LOW)
+                    for k, cut in enumerate(cuts)
+                ]
+            old = m_s[j, rows, :]
+            best = functools.reduce(jnp.maximum, cuts)
+            top = jnp.maximum(
+                old, jnp.broadcast_to(jnp.max(best, axis=1, keepdims=True), (CHUNK, HD))
+            )
+            for k, cut in enumerate(cuts):
+                weights[rows, k * HD : (k + 1) * HD] = jnp.exp2(cut - top).astype(BF16)
+            shrink = jnp.exp2(old - top)
+            m_s[j, rows, :] = top
+            acc[j, rows, 0:HD] = acc[j, rows, 0:HD] * shrink
+            acc[j, rows, HD:] = acc[j, rows, HD:] * shrink
+        acc[j] += jnp.dot(weights[:, 0:width], va_s[two, side, :], preferred_element_type=F32)
+
+    def run(n, item, ahead=None):
         @pl.when(n > 0)
         def _():
             score(item(0), sa_s)
 
         def two(t, carry):
             score(item(2 * t + 1), sb_s)
-            absorb(item(2 * t), sa_s, masked)
+            absorb(item(2 * t), sa_s, pa_s, ahead)
             score(item(jnp.minimum(2 * t + 2, n - 1)), sa_s)
-            absorb(item(2 * t + 1), sb_s, masked)
+            absorb(item(2 * t + 1), sb_s, pb_s, ahead)
             return carry
 
         lax.fori_loop(0, n // 2, two, 0)
 
         @pl.when(n % 2 == 1)
         def _():
-            absorb(item(n - 1), sa_s, masked)
+            absorb(item(n - 1), sa_s, pa_s, ahead)
 
     own = jnp.where(low, TILES, TILES - count)
-    every = jnp.where(low, TILES + count, own)
-
-    prepare(0, g)
-    run(own, lambda t: (t, 0), True)
-
-    def slot_at(i):
-        near = sum(jnp.where(i == e, ORDER[e][0], 0) for e in range(16))
-        far = sum(jnp.where(i == e, ORDER[e][1], 0) for e in range(16))
-        return slot_of(near, far)
-
-    def block(i, carry):
-        for turn, events in enumerate(TURNS):
-
-            @pl.when(i == turn + 1)
+    taken = jnp.where(low, count, 0)
+
+    prepare(g)
+    run(own, lambda t: (t, g, False), 0)
+
+    def finish(j, h):
+        rows = slice(h * TILE_TOK, (h + 1) * TILE_TOK)
+        return (acc[j, rows, 0:HD] / acc[j, rows, HD:]).astype(BF16)
+
+    def pair_at(i):
+        half = i // 4
+        step = jnp.where(core == 0, i % 4, i // 2)
+        across = jnp.where(core == 0, 1 - half, 1 - i % 2)
+        near = jnp.where(step == 0, 0, jnp.where(step == 1, 3, step - 1))
+        return ((x + near) % 4) * 2 + (y + across) % 2
+
+    def prepare_pair(i):
+        for side in range(2):
+            slot = 2 * pair_at(i) + side
+
+            @pl.when(slot <= last)
+            def _():
+                prepare(slot)
+
+    def turn(i, carry):
+        for at, events in enumerate(TURNS):
+
+            @pl.when(i == at)
             def _():
                 for e in events:
                     arrive(ORDER[e])
 
-        @pl.when(i == JOIN)
-        def _():
+        @pl.when(i < PAIRS // 2)
+        def _():
+            prepare_pair(i)
+
+        @pl.when(i == PAIRS // 2)
+        def _():
+            def rest(k, carry):
+                prepare_pair(k)
+                return carry
+
+            lax.fori_loop(PAIRS // 2, PAIRS, rest, 0)
             for t in range(LENT):
                 for n in range(QN):
 
@@ -369,69 +408,35 @@
                     def _():
                         lend(t, n).wait_recv()
 
-        slot = slot_at(i)
-        joined = (i >= JOIN) & (i <= EARLY)
-
-        @pl.when(slot <= last)
-        def _():
-            prepare(i, slot)
-
-        start = jnp.where(slot < g, 0, TILES)
-        stop = jnp.where(joined, every, own)
-        n = jnp.where(slot < last, jnp.maximum(stop - start, 0), 0)
-        run(n, lambda t: (start + t, i), False)
-
-        @pl.when(joined & (slot == last))
-        def _():
-            run(every - TILES, lambda t: (TILES + t, i), True)
-
+            def single(k, carry):
+                start = jnp.where(k == 2, 0, TILES)
+                odd = jnp.where(k == 2, g, last) % 2
+                n = jnp.where(k == 0, taken, odd * jnp.where(k == 1, taken, own))
+                block = jnp.where(k == 0, last, jnp.where(k == 1, last, g) - 1)
+                run(n, lambda t: (start + t, block, False), jnp.where(k == 0, 0, TOK))
+                return carry
+
+            lax.fori_loop(0, 3, single, 0)
+
+            def away(j, carry):
+                run(last // 2, lambda t: (j, t, True))
+                for h in range(HEADS):
+                    of_s[j - TILES, :, h * HD : (h + 1) * HD] = finish(j, h)
+                for f in range(LENT):
+
+                    @pl.when(j == TILES + f)
+                    def _():
+                        give_back(f).start()
+
+                return carry
+
+            lax.fori_loop(TILES, TILES + taken, away, 0)
+
+        two = pair_at(i)
+        run(jnp.where(two < g // 2, own, 0), lambda t: (t, two, True))
         return carry
 
-    lax.fori_loop(1, EARLY + 1, block, 0)
-
-    def prepare_late(i, carry):
-        slot = slot_at(i)
-
-        @pl.when(slot <= last)
-        def _():
-            prepare(i, slot)
-
-        return carry
-
-    lax.fori_loop(EARLY + 1, 16, prepare_late, 0)
-
-    def finish(j, h):
-        rows = slice(h * TILE_TOK, (h + 1) * TILE_TOK)
-        return (acc[j, rows, 0:HD] / acc[j, rows, HD:]).astype(BF16)
-
-    due = [e for e in range(16) if e < JOIN or e > EARLY]
-    wanted = [jnp.where(slot_of(*ORDER[e]) < last, 1, 0) for e in due]
-    before = [sum(wanted[:k], jnp.int32(0)) for k in range(len(due))]
-
-    def due_at(t):
-        return sum(
-            jnp.where((wanted[k] == 1) & (before[k] == t), due[k], 0) for k in range(len(due))
-        )
-
-    def late(j, carry):
-        run(before[-1] + wanted[-1], lambda t: (j, due_at(t)), False)
-        for h in range(HEADS):
-            of_s[j - TILES, :, h * HD : (h + 1) * HD] = finish(j, h)
-        for f in range(LENT):
-
-            @pl.when(j == TILES + f)
-            def _():
-                give_back(f).start()
-
-        return carry
-
-    lax.fori_loop(TILES, every, late, 0)
-
-    def late_own(i, carry):
-        run(jnp.where(slot_at(i) < g, own, 0), lambda t: (t, i), False)
-        return carry
-
-    lax.fori_loop(EARLY + 1, 16, late_own, 0)
+    lax.fori_loop(0, PAIRS, turn, 0)
 
     for j in range(TILES):
 
@@ -470,82 +475,71 @@
 def decode(
     table, lens, dest, pre_in, cache, dq, dkv, new,
     pre_out, dec_out,
-    cf_s, sd_s, sem,
+    pre_s, pool_s, mix_s, page_s, dq_s, out_s, in_sem, out_sem, pool_sem,
 ):
-    hand_on = pltpu.make_async_copy(pre_in, pre_out, sem)
-    hand_on.start()
-    cf_s[...] = cache[...].astype(F32)
-    tokens = PAGES * PAGE
-
-    lane = lax.broadcasted_iota(jnp.int32, (1, PAGES), 1)
-    limits = []
+    half = TOK // 2
+
+    def take(k):
+        rows = pl.ds(k * half, half)
+        return pltpu.make_async_copy(pre_in.at[rows, :], pre_s.at[rows, :], in_sem.at[k])
+
+    def hand_on(k):
+        rows = pl.ds(k * half, half)
+        return pltpu.make_async_copy(pre_s.at[rows, :], pre_out.at[rows, :], out_sem.at[k])
+
+    pool = pltpu.make_async_copy(cache, page_s, pool_sem)
+    pool.start()
+    for k in range(2):
+        take(k).start()
+
+    mix_s[pl.ds(0, NEW_ROWS, stride=2), :] = new[0].astype(F32)
+    mix_s[pl.ds(1, NEW_ROWS, stride=2), :] = new[1].astype(F32)
+    pool.wait()
+    for m in range(TOK // PAGE):
+        at = pl.ds(pl.multiple_of(dest[0, m] * 2 * PAGE, 2 * PAGE), 2 * PAGE)
+        page_s[at, :] = mix_s[m * 2 * PAGE : (m + 1) * 2 * PAGE, :].astype(BF16)
+    dq_s[...] = dq[...].astype(F32)
     for r in range(ROWS):
-        limit = jnp.zeros((1, PAGES), jnp.int32)
         for j in range(MAXP):
-            left = jnp.clip(lens[r] - j * PAGE, 0, PAGE)
-            limit = jnp.where(lane == table[r, j], left, limit)
-        limits.append(limit)
-    limit = jnp.concatenate(limits, axis=0).astype(F32)
-    new_page = lax.broadcasted_iota(jnp.int32, (1, NEW_ROWS), 1) >> 4
-    new_slot = jnp.zeros((1, NEW_ROWS), jnp.int32)
-    replaced = jnp.zeros((1, PAGES), jnp.int32)
-    for m in range(TOK // PAGE):
-        new_slot = jnp.where(new_page == m, dest[0, m], new_slot)
-        replaced = jnp.where(lane == dest[0, m], 1, replaced)
-    old_limit = jnp.where(replaced == 1, 0.0, limit).astype(BF16)
-
-    def bias(limit, page):
-        total = page.shape[1]
-        pick = jnp.where(
-            lax.broadcasted_iota(jnp.int32, (PAGES, total), 0) == page, 1.0, 0.0
+            at = pl.ds(pl.multiple_of(table[r, j] * 2 * PAGE, 2 * PAGE), 2 * PAGE)
+            pool_s[r, j * 2 * PAGE : (j + 1) * 2 * PAGE, :] = page_s[at, :]
+
+    for k in range(2):
+        take(k).wait()
+        hand_on(k).start()
+
+    wide = 2 * MAXP * PAGE
+    queries = HEADS * STEPS
+    column = lax.broadcasted_iota(jnp.int32, (queries, wide), 1)
+    query = lax.broadcasted_iota(jnp.int32, (queries, DEC), 0)
+    token = lax.broadcasted_iota(jnp.int32, (queries, DEC), 1)
+    so_far = (token >> 3) <= (query & (STEPS - 1))
+    for r in range(ROWS):
+        q = dq_s[pl.ds(r, queries, stride=ROWS), :].astype(BF16)
+
+        def scores(keys):
+            return lax.dot_general(q, keys, (((1,), (1,)), ((), ())), preferred_element_type=F32)
+
+        live = ((column & 1) == 0) & (column < 2 * lens[r])
+        s_old = jnp.where(live, scores(pool_s[r]), LOW)
+        s_new = jnp.where(so_far & ((token & (ROWS - 1)) == r), scores(dkv[0]), LOW)
+        top = jnp.maximum(
+            jnp.max(s_old, axis=1, keepdims=True), jnp.max(s_new, axis=1, keepdims=True)
+        )
+        p_old = jnp.exp2(s_old - top)
+        p_new = jnp.exp2(s_new - top)
+        total = jnp.sum(p_old, axis=1, keepdims=True) + jnp.sum(p_new, axis=1, keepdims=True)
+        p_old = jnp.concatenate(
+            [pltpu.roll(p_old[:, k * HD : (k + 1) * HD], 1, 1) for k in range(wide // HD)], axis=1
         ).astype(BF16)
-        held = jnp.dot(limit, pick, preferred_element_type=F32)
-        offset = lax.broadcasted_iota(jnp.int32, (1, total), 1) & (PAGE - 1)
-        return jnp.where(offset.astype(F32) < held, 0.0, LOW)
-
-    def scores(keys):
-        return lax.dot_general(
-            dq[...], keys, (((1,), (1,)), ((), ())), preferred_element_type=F32
-        )
-
-    def over_queries(mask):
-        return jnp.broadcast_to(mask[None], (HEADS * STEPS, *mask.shape)).reshape(
-            HEADS * DEC, mask.shape[1]
-        )
-
-    query_row = lax.broadcasted_iota(jnp.int32, (HEADS * DEC, DEC), 0)
-    key_row = lax.broadcasted_iota(jnp.int32, (HEADS * DEC, DEC), 1)
-    tok_ok = ((query_row & (ROWS - 1)) == (key_row & (ROWS - 1))) & (
-        (key_row >> 3) <= ((query_row & (DEC - 1)) >> 3)
-    )
-    part = 512
-    parts = tokens // part
-    s_tok = jnp.where(tok_ok, scores(dkv[0]), LOW)
-    top = jnp.max(s_tok, axis=1, keepdims=True)
-    s_new = scores(new[0]) + over_queries(bias(limit.astype(BF16), new_slot))
-    top = jnp.maximum(top, jnp.max(s_new, axis=1, keepdims=True))
-    for i in range(parts):
-        cols = slice(i * part, (i + 1) * part)
-        page = (lax.broadcasted_iota(jnp.int32, (1, part), 1) >> 4) + i * (part // PAGE)
-        keys = cf_s[pl.ds(2 * i * part, part, stride=2), :].astype(BF16)
-        s_old = scores(keys) + over_queries(bias(old_limit, page))
-        sd_s[:, cols] = s_old
-        top = jnp.maximum(top, jnp.max(s_old, axis=1, keepdims=True))
-    p = jnp.exp2(s_tok - top)
-    total = jnp.sum(p, axis=1, keepdims=True)
-    mixed = jnp.dot(p.astype(BF16), dkv[1], preferred_element_type=F32)
-    p = jnp.exp2(s_new - top)
-    total = total + jnp.sum(p, axis=1, keepdims=True)
-    mixed = mixed + jnp.dot(p.astype(BF16), new[1], preferred_element_type=F32)
-    for i in range(parts):
-        p = jnp.exp2(sd_s[:, i * part : (i + 1) * part] - top)
-        total = total + jnp.sum(p, axis=1, keepdims=True)
-        values = cf_s[pl.ds(2 * i * part + 1, part, stride=2), :].astype(BF16)
-        mixed = mixed + jnp.dot(p.astype(BF16), values, preferred_element_type=F32)
-    mixed = mixed / total
+        mixed = jnp.dot(p_old, pool_s[r], preferred_element_type=F32) + jnp.dot(
+            p_new.astype(BF16), dkv[1], preferred_element_type=F32
+        )
+        out_s[pl.ds(r, queries, stride=ROWS), :] = mixed / total
     for h in range(HEADS):
-        dec_out[:, h * HD : (h + 1) * HD] = mixed[h * DEC : (h + 1) * DEC, :].astype(BF16)
-    hand_on.wait()
+        dec_out[:, h * HD : (h + 1) * HD] = out_s[h * DEC : (h + 1) * DEC, :].astype(BF16)
+    for k in range(2):
+        hand_on(k).wait()
 
 
 def per_device(pre_x, w_query, w_key, w_value, dec_x, cache, lengths, page_table, dest_slots):
@@ -567,15 +561,17 @@
             pltpu.VMEM((D, 2 * HD), BF16),
             pltpu.VMEM((D, HEADS * HD), BF16),
             pltpu.VMEM((GROUPS, 2, TOK, HD), BF16),
-            pltpu.VMEM((GROUPS, HD, TOK), BF16),
-            pltpu.VMEM((GROUPS, TOK, 2 * HD), BF16),
+            pltpu.VMEM((PAIRS, HD, 2 * TOK), BF16),
+            pltpu.VMEM((PAIRS, 2 * TOK, 2 * HD), BF16),
             pltpu.VMEM((LENT, TILE_TOK, HEADS * HD), BF16),
             pltpu.VMEM((TILES + LENT, TILE, HD), BF16),
             pltpu.VMEM((ALL, HEADS * HD // QN), F32),
             pltpu.VMEM((TILES + LENT, TILE, 2 * HD), F32),
             pltpu.VMEM((TILES + LENT, TILE, HD), F32),
-            pltpu.VMEM((TILE, TOK), F32),
-            pltpu.VMEM((TILE, TOK), F32),
+            pltpu.VMEM((TILE, 2 * TOK), F32),
+            pltpu.VMEM((TILE, 2 * TOK), F32),
+            pltpu.VMEM((TILE, 2 * TOK), BF16),
+            pltpu.VMEM((TILE, 2 * TOK), BF16),
             pltpu.SemaphoreType.DMA((XC,)),
             pltpu.SemaphoreType.DMA((XC,)),
             pltpu.SemaphoreType.DMA((XC,)),
@@ -600,11 +596,17 @@
             jax.ShapeDtypeStruct((TOK, HEADS * HD), BF16),
             jax.ShapeDtypeStruct((DEC, HEADS * HD), BF16),
         ),
-        in_specs=[smem] * 3 + [hbm] + [vmem] * 4,
+        in_specs=[smem] * 3 + [hbm] * 2 + [vmem] * 3,
         out_specs=(hbm, vmem),
         scratch_shapes=[
-            pltpu.VMEM((CACHE_ROWS, HD), F32),
-            pltpu.VMEM((HEADS * DEC, PAGES * PAGE), F32),
+            pltpu.VMEM((TOK, HEADS * HD), BF16),
+            pltpu.VMEM((ROWS, 2 * MAXP * PAGE, HD), BF16),
+            pltpu.VMEM((2 * NEW_ROWS, HD), F32),
+            pltpu.VMEM((CACHE_ROWS, HD), BF16),
+            pltpu.VMEM((HEADS * DEC, HD), F32),
+            pltpu.VMEM((HEADS * DEC, HD), F32),
+            pltpu.SemaphoreType.DMA((2,)),
+            pltpu.SemaphoreType.DMA((2,)),
             pltpu.SemaphoreType.DMA,
         ],
         compiler_params=pltpu.CompilerParams(vmem_limit_bytes=63 * 1024 * 1024),

time: 118 us -> 87.5 us (0.74)
  Pallas kernels: 117 us -> 86.6 us
    pallas_call x1, Pallas kernels: 34.8 us -> 6 us  [per_device(): pl.pallas_call(decode, out_shape=(jax.ShapeDtypeStruct((TOK, HEADS * HD),...]
    pallas_call x1, Pallas kernels: 82.3 us -> 80.6 us  [per_device(): pl.pallas_call(prefill, out_shape=(jax.ShapeDtypeStruct((TOK, HEADS * HD)...]
where the time goes in v2:
time: 87.5 us; the launch traced here: 87.4 us
  Pallas kernels  86.6 us (99%)
    pallas_call x1, Pallas kernels, per_device(): pl.pallas_call(prefill, out_shape=(jax.ShapeDtypeStruct((TOK, HEADS * HD)...  80.6 us
    pallas_call x1, Pallas kernels, per_device(): pl.pallas_call(decode, out_shape=(jax.ShapeDtypeStruct((TOK, HEADS * HD),...  6 us

profile of v2, /device:TPU:30, one launch (start us, length us, event | category | flops | bytes accessed | tf_op | source)
XLA Modules:
  0.0 87.4 jit_solution(5522103856578179891)
XLA Ops:
  0.6 80.6 %shard_map.104 = (bf16[512,1024]{1,0:T(8,128)(2,1)}, bf16[256,128]{1,0:T(8,128)(2,1)}, bf16[2,32,128]{2,1,0:T(8,128)(2,1)}, bf16[2,512,128]{2,1,0:T(8,128)(2,1)}) custom-call(bf16[512,8192]{1,0:T(8,128)(2,1)} %px.1, bf16[8192,1024]{1,0:T(8,128)(2,1)} %wq.1, bf16[8192,128]{1,0:T(8,128)(2,1)} %wk.1, bf16[8192,128]{1,0:T(8,128)(2,1)} %wv.1, ...), custom_call_target="tpu_custom_call" | custom-call | tf_op jit(solution)/shard_map/pallas_call | solution.py:549
  81.2 6.0 %shard_map.105 = (bf16[512,1024]{1,0:T(8,128)(2,1)}, bf16[32,1024]{1,0:T(8,128)(2,1)}) custom-call(s32[8,16]{1,0:T(8,128)} %table.1, s32[8]{0:T(128)} %lens.1, s32[1,32]{1,0:T(1,128)} %dest.1, bf16[512,1024]{1,0:T(8,128)(2,1)} %get-tuple-element.8.pre_in, bf16[4096,128]{1,0:T(8,128)(2,1)} %bitcast.3, bf16[256,128]{1,0:T(8,128)(2,1)} %get-tuple-element.9.dq, ...), custom_call_target="tpu_custom_call" | custom-call | tf_op jit(solution)/shard_map/pallas_call | solution.py:593

commit v3 on v2

--- a/solution.py
+++ b/solution.py
@@ -31,13 +31,15 @@
 SCALE = HD ** (-0.5) * 1.4426950408889634
 LOW = -1e30
 XC = 8
-QK = 4
-QN = 2
+QK = 2
+QN = 4
 LENT = 4
 TAKES = (4, 3, 3, 2, 2, 1, 1, 0)
 PAIRS = GROUPS // 2
 CHUNK = 16
-TURNS = ((), (6, 7), (8, 9), (10, 11), (12, 13, 14, 15))
+HALF = TILE // 2
+SHIFT = 4.0
+POLLS = {2: (1, 2), 4: (5,), 5: (3, 4), 7: (6, 7)}
 
 ORDER = (
     (0, 0), (3, 0), (1, 0), (0, 3), (0, 1), (2, 0), (3, 3), (3, 1),
@@ -77,7 +79,7 @@
 def prefill(
     px, wq, wk, wv, dx,
     pre_out, dq_out, dkv_out, new_out,
-    x_s, wkv_s, wq_s, kv_s, kt_s, va_s, of_s, q_s, pacc, acc, m_s, sa_s, sb_s, pa_s, pb_s,
+    x_s, wkv_s, wq_s, kv_s, kt_s, va_s, of_s, q_s, pacc, acc, m_s, sa_s, sb_s, pa_s, pb_s, ha_s, hb_s,
     xsem, wksem, wvsem, qsem, dsem_own, dsend, drecv, ssem, rsem, qsend, qrecv, osend, orecv,
 ):
     seq, tensor, pool = lax.axis_index("seq"), lax.axis_index("tensor"), lax.axis_index("pool")
@@ -271,6 +273,8 @@
                 pacc[...] = part
             else:
                 pacc[...] += part
+            for e in POLLS.get(n * QK + k, ()):
+                arrive(ORDER[e])
         for hh in range(HEADS // QN):
             h = n * (HEADS // QN) + hh
             for j in range(TILES):
@@ -286,15 +290,9 @@
             def _():
                 lend(t, n).start()
 
-        if n == 0:
-            arrive(ORDER[1])
-            arrive(ORDER[2])
     dkv = jnp.dot(x_s[TOK:ALL, :], wkv_s[...], preferred_element_type=F32)
     dkv_out[0] = dkv[:, 0:HD].astype(BF16)
     dkv_out[1] = dkv[:, HD : 2 * HD].astype(BF16)
-
-    for event in ORDER[3:6]:
-        arrive(event)
 
     def prepare(slot):
         side = pl.ds(pl.multiple_of((slot % 2) * TOK, TOK), TOK)
@@ -307,61 +305,108 @@
             return j, block, slice(0, 2 * TOK), 2 * TOK
         return j, block // 2, pl.ds(pl.multiple_of((block % 2) * TOK, TOK), TOK), TOK
 
-    def score(item, buf):
+    def weave(*streams):
+        steps = [
+            ((k + 0.5) / len(stream), number, step)
+            for number, stream in enumerate(streams)
+            for k, step in enumerate(stream)
+        ]
+        for _, _, step in sorted(steps, key=lambda at: at[:2]):
+            step()
+
+    bufs = ((sa_s, pa_s, ha_s), (sb_s, pb_s, hb_s))
+
+    def score(item, half):
         j, two, side, width = part_of(item)
-        buf[:, 0:width] = jnp.dot(q_s[j], kt_s[two, :, side], preferred_element_type=F32)
-
-    def absorb(item, buf, weights, ahead):
+        buf = bufs[half][0]
+        rows = slice(half * HALF, (half + 1) * HALF)
+        at = 0 if width == 2 * TOK else pl.multiple_of((item[1] % 2) * TOK, TOK)
+
+        def step(n):
+            keys = kt_s[two, :, pl.ds(at + n * 2 * HD, 2 * HD)]
+            buf[:, n * 2 * HD : (n + 1) * 2 * HD] = jnp.dot(
+                q_s[j, rows, :], keys, preferred_element_type=F32
+            )
+
+        return [functools.partial(step, n) for n in range(width // (2 * HD))]
+
+    def weigh(item, half, ahead):
         j, two, side, width = part_of(item)
+        buf, weights, shrinks = bufs[half]
         if ahead is not None:
             first = jnp.where(j < TILES, j, j - count) * TILE_TOK + ahead
             lead = lax.broadcasted_iota(jnp.int32, (CHUNK, HD), 1) - lax.broadcasted_iota(
                 jnp.int32, (CHUNK, HD), 0
             )
-        for c in range(TILE // CHUNK):
+
+        def step(c):
             rows = slice(c * CHUNK, (c + 1) * CHUNK)
+            whole = slice(half * HALF + c * CHUNK, half * HALF + (c + 1) * CHUNK)
             cuts = [buf[rows, k * HD : (k + 1) * HD] for k in range(width // HD)]
             if ahead is not None:
                 cuts = [
                     jnp.where(lead <= first + (c * CHUNK % TILE_TOK - k * HD), cut, LOW)
                     for k, cut in enumerate(cuts)
                 ]
-            old = m_s[j, rows, :]
+            old = m_s[j, whole, :]
             best = functools.reduce(jnp.maximum, cuts)
             top = jnp.maximum(
-                old, jnp.broadcast_to(jnp.max(best, axis=1, keepdims=True), (CHUNK, HD))
+                old, jnp.broadcast_to(jnp.max(best, axis=1, keepdims=True) - SHIFT, (CHUNK, HD))
             )
             for k, cut in enumerate(cuts):
-                weights[rows, k * HD : (k + 1) * HD] = jnp.exp2(cut - top).astype(BF16)
-            shrink = jnp.exp2(old - top)
-            m_s[j, rows, :] = top
-            acc[j, rows, 0:HD] = acc[j, rows, 0:HD] * shrink
-            acc[j, rows, HD:] = acc[j, rows, HD:] * shrink
-        acc[j] += jnp.dot(weights[:, 0:width], va_s[two, side, :], preferred_element_type=F32)
+                weights[rows, k * HD : (k + 1) * HD] = jnp.exp2((cut - top).astype(BF16))
+            shrinks[rows, :] = jnp.exp2(old - top)
+            m_s[j, whole, :] = top
+
+        return [functools.partial(step, c) for c in range(HALF // CHUNK)]
+
+    def collect(item, half):
+        j, two, side, width = part_of(item)
+        _, weights, shrinks = bufs[half]
+
+        o = jnp.dot(weights[:, 0:width], va_s[two, side, :], preferred_element_type=F32)
+        for c in range(HALF // CHUNK):
+            rows = slice(c * CHUNK, (c + 1) * CHUNK)
+            whole = slice(half * HALF + c * CHUNK, half * HALF + (c + 1) * CHUNK)
+            shrink = shrinks[rows, :]
+            acc[j, whole, 0:HD] = acc[j, whole, 0:HD] * shrink + o[rows, 0:HD]
+            acc[j, whole, HD:] = acc[j, whole, HD:] * shrink + o[rows, HD:]
 
     def run(n, item, ahead=None):
         @pl.when(n > 0)
         def _():
-            score(item(0), sa_s)
-
-        def two(t, carry):
-            score(item(2 * t + 1), sb_s)
-            absorb(item(2 * t), sa_s, pa_s, ahead)
-            score(item(jnp.minimum(2 * t + 2, n - 1)), sa_s)
-            absorb(item(2 * t + 1), sb_s, pb_s, ahead)
-            return carry
-
-        lax.fori_loop(0, n // 2, two, 0)
-
-        @pl.when(n % 2 == 1)
-        def _():
-            absorb(item(n - 1), sa_s, pa_s, ahead)
+            weave(score(item(0), 0))
+            weave(score(item(0), 1), weigh(item(0), 0, ahead))
+
+            def one(t, carry):
+                now, later = item(t), item(t + 1)
+                collect(now, 0)
+                weave(score(later, 0), weigh(now, 1, ahead))
+                collect(now, 1)
+                weave(score(later, 1), weigh(later, 0, ahead))
+                return carry
+
+            lax.fori_loop(0, n - 1, one, 0)
+            collect(item(n - 1), 0)
+            weave(weigh(item(n - 1), 1, ahead))
+            collect(item(n - 1), 1)
 
     own = jnp.where(low, TILES, TILES - count)
     taken = jnp.where(low, count, 0)
 
     prepare(g)
-    run(own, lambda t: (t, g, False), 0)
+    def begin(k, carry):
+        run(own // 2 + k * (own % 2), lambda t: (t + k * (own // 2), g, False), 0)
+        for at, events in enumerate(((8, 9), (10, 11))):
+
+            @pl.when(k == at)
+            def _():
+                for e in events:
+                    arrive(ORDER[e])
+
+        return carry
+
+    lax.fori_loop(0, 2, begin, 0)
 
     def finish(j, h):
         rows = slice(h * TILE_TOK, (h + 1) * TILE_TOK)
@@ -383,19 +428,15 @@
                 prepare(slot)
 
     def turn(i, carry):
-        for at, events in enumerate(TURNS):
-
-            @pl.when(i == at)
-            def _():
-                for e in events:
-                    arrive(ORDER[e])
-
         @pl.when(i < PAIRS // 2)
         def _():
             prepare_pair(i)
 
         @pl.when(i == PAIRS // 2)
         def _():
+            for e in (12, 13, 14, 15):
+                arrive(ORDER[e])
+
             def rest(k, carry):
                 prepare_pair(k)
                 return carry
@@ -568,10 +609,12 @@
             pltpu.VMEM((ALL, HEADS * HD // QN), F32),
             pltpu.VMEM((TILES + LENT, TILE, 2 * HD), F32),
             pltpu.VMEM((TILES + LENT, TILE, HD), F32),
-            pltpu.VMEM((TILE, 2 * TOK), F32),
-            pltpu.VMEM((TILE, 2 * TOK), F32),
-            pltpu.VMEM((TILE, 2 * TOK), BF16),
-            pltpu.VMEM((TILE, 2 * TOK), BF16),
+            pltpu.VMEM((HALF, 2 * TOK), F32),
+            pltpu.VMEM((HALF, 2 * TOK), F32),
+            pltpu.VMEM((HALF, 2 * TOK), BF16),
+            pltpu.VMEM((HALF, 2 * TOK), BF16),
+            pltpu.VMEM((HALF, HD), F32),
+            pltpu.VMEM((HALF, HD), F32),
             pltpu.SemaphoreType.DMA((XC,)),
             pltpu.SemaphoreType.DMA((XC,)),
             pltpu.SemaphoreType.DMA((XC,)),

time: 87.5 us -> 91.5 us (1.046)
  Pallas kernels: 86.6 us -> 90.6 us
    pallas_call x1, Pallas kernels: 80.6 us -> 84.6 us  [per_device(): pl.pallas_call(prefill, out_shape=(jax.ShapeDtypeStruct((TOK, HEADS * HD)...]
where the time goes in v3:
time: 91.5 us; the launch traced here: 91.4 us
  Pallas kernels  90.6 us (99%)
    pallas_call x1, Pallas kernels, per_device(): pl.pallas_call(prefill, out_shape=(jax.ShapeDtypeStruct((TOK, HEADS * HD)...  84.6 us
    pallas_call x1, Pallas kernels, per_device(): pl.pallas_call(decode, out_shape=(jax.ShapeDtypeStruct((TOK, HEADS * HD),...  6 us

profile of v3, /device:TPU:30, one launch (start us, length us, event | category | flops | bytes accessed | tf_op | source)
XLA Modules:
  0.0 91.4 jit_solution(5529311645443909846)
XLA Ops:
  0.6 84.6 %shard_map.104 = (bf16[512,1024]{1,0:T(8,128)(2,1)}, bf16[256,128]{1,0:T(8,128)(2,1)}, bf16[2,32,128]{2,1,0:T(8,128)(2,1)}, bf16[2,512,128]{2,1,0:T(8,128)(2,1)}) custom-call(bf16[512,8192]{1,0:T(8,128)(2,1)} %px.1, bf16[8192,1024]{1,0:T(8,128)(2,1)} %wq.1, bf16[8192,128]{1,0:T(8,128)(2,1)} %wk.1, bf16[8192,128]{1,0:T(8,128)(2,1)} %wv.1, ...), custom_call_target="tpu_custom_call" | custom-call | tf_op jit(solution)/shard_map/pallas_call | solution.py:590
  85.2 6.0 %shard_map.105 = (bf16[512,1024]{1,0:T(8,128)(2,1)}, bf16[32,1024]{1,0:T(8,128)(2,1)}) custom-call(s32[8,16]{1,0:T(8,128)} %table.1, s32[8]{0:T(128)} %lens.1, s32[1,32]{1,0:T(1,128)} %dest.1, bf16[512,1024]{1,0:T(8,128)(2,1)} %get-tuple-element.8.pre_in, bf16[4096,128]{1,0:T(8,128)(2,1)} %bitcast.3, bf16[256,128]{1,0:T(8,128)(2,1)} %get-tuple-element.9.dq, ...), custom_call_target="tpu_custom_call" | custom-call | tf_op jit(solution)/shard_map/pallas_call | solution.py:636

commit v4 on v2

--- a/solution.py
+++ b/solution.py
@@ -34,10 +34,12 @@
 QK = 4
 QN = 2
 LENT = 4
-TAKES = (4, 3, 3, 2, 2, 1, 1, 0)
+TAKES = (3, 3, 3, 3, 2, 2, 1, 0)
 PAIRS = GROUPS // 2
 CHUNK = 16
-TURNS = ((), (6, 7), (8, 9), (10, 11), (12, 13, 14, 15))
+POLLS = {5: (1, 2), 7: (3, 4, 5)}
+TURNS = {1: (6, 7, 8, 9), 2: (10, 11), 4: (12, 13, 14, 15)}
+JOIN, PART = 2, 6
 
 ORDER = (
     (0, 0), (3, 0), (1, 0), (0, 3), (0, 1), (2, 0), (3, 3), (3, 1),
@@ -126,9 +128,6 @@
         w_copy(c, wk, 0, wksem).start()
         w_copy(c, wv, HD, wvsem).start()
     dec_own.start()
-    for n in range(QN):
-        for k in range(QK):
-            q_copy(n, k).start()
 
     barrier = pltpu.get_barrier_semaphore()
     for way in ways.values():
@@ -237,6 +236,12 @@
         x_copy(c).wait()
         w_copy(c, wk, 0, wksem).wait()
         w_copy(c, wv, HD, wvsem).wait()
+        for k in range(QN * QK):
+
+            @pl.when(c == 4 + k // 2)
+            def _():
+                q_copy(k // QK, k % QK).start()
+
         at = pl.ds(pl.multiple_of(c * (D // XC), D // XC), D // XC)
         part = jnp.dot(x_s[0:TOK, at], wkv_s[at, :], preferred_element_type=F32)
 
@@ -271,6 +276,8 @@
                 pacc[...] = part
             else:
                 pacc[...] += part
+            for e in POLLS.get(n * QK + k, ()):
+                arrive(ORDER[e])
         for hh in range(HEADS // QN):
             h = n * (HEADS // QN) + hh
             for j in range(TILES):
@@ -286,15 +293,9 @@
             def _():
                 lend(t, n).start()
 
-        if n == 0:
-            arrive(ORDER[1])
-            arrive(ORDER[2])
     dkv = jnp.dot(x_s[TOK:ALL, :], wkv_s[...], preferred_element_type=F32)
     dkv_out[0] = dkv[:, 0:HD].astype(BF16)
     dkv_out[1] = dkv[:, HD : 2 * HD].astype(BF16)
-
-    for event in ORDER[3:6]:
-        arrive(event)
 
     def prepare(slot):
         side = pl.ds(pl.multiple_of((slot % 2) * TOK, TOK), TOK)
@@ -382,31 +383,38 @@
             def _():
                 prepare(slot)
 
+    due = [i for i in range(PAIRS) if i < JOIN or i >= PART]
+    wanted = [jnp.where(pair_at(i) < last // 2, 1, 0) for i in due]
+    before = [sum(wanted[:k], jnp.int32(0)) for k in range(len(due))]
+
+    def due_at(t):
+        return sum(
+            jnp.where((wanted[k] == 1) & (before[k] == t), pair_at(due[k]), 0)
+            for k in range(len(due))
+        )
+
     def turn(i, carry):
-        for at, events in enumerate(TURNS):
+        for at, events in TURNS.items():
 
             @pl.when(i == at)
             def _():
                 for e in events:
                     arrive(ORDER[e])
 
-        @pl.when(i < PAIRS // 2)
-        def _():
-            prepare_pair(i)
-
-        @pl.when(i == PAIRS // 2)
-        def _():
-            def rest(k, carry):
-                prepare_pair(k)
-                return carry
-
-            lax.fori_loop(PAIRS // 2, PAIRS, rest, 0)
+        @pl.when(i == JOIN)
+        def _():
             for t in range(LENT):
                 for n in range(QN):
 
                     @pl.when(low & lent(t))
                     def _():
                         lend(t, n).wait_recv()
+
+        prepare_pair(i)
+
+        @pl.when(i == PART)
+        def _():
+            prepare_pair(PART + 1)
 
             def single(k, carry):
                 start = jnp.where(k == 2, 0, TILES)
@@ -419,7 +427,7 @@
             lax.fori_loop(0, 3, single, 0)
 
             def away(j, carry):
-                run(last // 2, lambda t: (j, t, True))
+                run(before[-1] + wanted[-1], lambda t: (j, due_at(t), True))
                 for h in range(HEADS):
                     of_s[j - TILES, :, h * HD : (h + 1) * HD] = finish(j, h)
                 for f in range(LENT):
@@ -433,7 +441,10 @@
             lax.fori_loop(TILES, TILES + taken, away, 0)
 
         two = pair_at(i)
-        run(jnp.where(two < g // 2, own, 0), lambda t: (t, two, True))
+        joined = (i >= JOIN) & (i < PART) & (two < last // 2)
+        start = jnp.where(two < g // 2, 0, TILES)
+        stop = jnp.where(joined & low, TILES + taken, own)
+        run(jnp.maximum(stop - start, 0), lambda t: (start + t, two, True))
         return carry
 
     lax.fori_loop(0, PAIRS, turn, 0)
@@ -514,6 +525,7 @@
     query = lax.broadcasted_iota(jnp.int32, (queries, DEC), 0)
     token = lax.broadcasted_iota(jnp.int32, (queries, DEC), 1)
     so_far = (token >> 3) <= (query & (STEPS - 1))
+    s_old, s_new = [], []
     for r in range(ROWS):
         q = dq_s[pl.ds(r, queries, stride=ROWS), :].astype(BF16)
 
@@ -521,21 +533,29 @@
             return lax.dot_general(q, keys, (((1,), (1,)), ((), ())), preferred_element_type=F32)
 
         live = ((column & 1) == 0) & (column < 2 * lens[r])
-        s_old = jnp.where(live, scores(pool_s[r]), LOW)
-        s_new = jnp.where(so_far & ((token & (ROWS - 1)) == r), scores(dkv[0]), LOW)
-        top = jnp.maximum(
-            jnp.max(s_old, axis=1, keepdims=True), jnp.max(s_new, axis=1, keepdims=True)
-        )
-        p_old = jnp.exp2(s_old - top)
-        p_new = jnp.exp2(s_new - top)
-        total = jnp.sum(p_old, axis=1, keepdims=True) + jnp.sum(p_new, axis=1, keepdims=True)
-        p_old = jnp.concatenate(
-            [pltpu.roll(p_old[:, k * HD : (k + 1) * HD], 1, 1) for k in range(wide // HD)], axis=1
+        s_old.append(jnp.where(live, scores(pool_s[r]), LOW))
+        s_new.append(jnp.where(so_far & ((token & (ROWS - 1)) == r), scores(dkv[0]), LOW))
+    tops = [
+        jnp.maximum(jnp.max(a, axis=1, keepdims=True), jnp.max(b, axis=1, keepdims=True))
+        for a, b in zip(s_old, s_new)
+    ]
+    p_old = [jnp.exp2(a - top) for a, top in zip(s_old, tops)]
+    p_new = [jnp.exp2(b - top) for b, top in zip(s_new, tops)]
+    totals = [
+        jnp.sum(a, axis=1, keepdims=True) + jnp.sum(b, axis=1, keepdims=True)
+        for a, b in zip(p_old, p_new)
+    ]
+    p_old = [
+        jnp.concatenate(
+            [pltpu.roll(a[:, k * HD : (k + 1) * HD], 1, 1) for k in range(wide // HD)], axis=1
         ).astype(BF16)
-        mixed = jnp.dot(p_old, pool_s[r], preferred_element_type=F32) + jnp.dot(
-            p_new.astype(BF16), dkv[1], preferred_element_type=F32
-        )
-        out_s[pl.ds(r, queries, stride=ROWS), :] = mixed / total
+        for a in p_old
+    ]
+    for r in range(ROWS):
+        mixed = jnp.dot(p_old[r], pool_s[r], preferred_element_type=F32) + jnp.dot(
+            p_new[r].astype(BF16), dkv[1], preferred_element_type=F32
+        )
+        out_s[pl.ds(r, queries, stride=ROWS), :] = mixed / totals[r]
     for h in range(HEADS):
         dec_out[:, h * HD : (h + 1) * HD] = out_s[h * DEC : (h + 1) * DEC, :].astype(BF16)
     for k in range(2):

time: 87.5 us -> 79.7 us (0.911)
  the two profiles are of different devices: /device:TPU:30 before, /device:TPU:12 now
where the time goes in v4:
time: 79.7 us; the launch traced here: 79.6 us
  Pallas kernels  78.8 us (99%)
  between operations  0.8 us (1%)
    pallas_call x1, Pallas kernels, per_device(): pl.pallas_call(prefill, out_shape=(jax.ShapeDtypeStruct((TOK, HEADS * HD)...  74.5 us
    pallas_call x1, Pallas kernels, per_device(): pl.pallas_call(decode, out_shape=(jax.ShapeDtypeStruct((TOK, HEADS * HD),...  4.25 us

profile of v4, /device:TPU:12, one launch (start us, length us, event | category | flops | bytes accessed | tf_op | source)
XLA Modules:
  0.0 79.6 jit_solution(1812308595457671243)
XLA Ops:
  0.6 74.5 %shard_map.104 = (bf16[512,1024]{1,0:T(8,128)(2,1)}, bf16[256,128]{1,0:T(8,128)(2,1)}, bf16[2,32,128]{2,1,0:T(8,128)(2,1)}, bf16[2,512,128]{2,1,0:T(8,128)(2,1)}) custom-call(bf16[512,8192]{1,0:T(8,128)(2,1)} %px.1, bf16[8192,1024]{1,0:T(8,128)(2,1)} %wq.1, bf16[8192,128]{1,0:T(8,128)(2,1)} %wk.1, bf16[8192,128]{1,0:T(8,128)(2,1)} %wv.1, ...), custom_call_target="tpu_custom_call" | custom-call | tf_op jit(solution)/shard_map/pallas_call | solution.py:569
  75.2 4.3 %shard_map.105 = (bf16[512,1024]{1,0:T(8,128)(2,1)}, bf16[32,1024]{1,0:T(8,128)(2,1)}) custom-call(s32[8,16]{1,0:T(8,128)} %table.1, s32[8]{0:T(128)} %lens.1, s32[1,32]{1,0:T(1,128)} %dest.1, bf16[512,1024]{1,0:T(8,128)(2,1)} %get-tuple-element.8.pre_in, bf16[4096,128]{1,0:T(8,128)(2,1)} %bitcast.3, bf16[256,128]{1,0:T(8,128)(2,1)} %get-tuple-element.9.dq, ...), custom_call_target="tpu_custom_call" | custom-call | tf_op jit(solution)/shard_map/pallas_call | solution.py:613

commit v5 on v4

--- a/solution.py
+++ b/solution.py
@@ -38,8 +38,9 @@
 PAIRS = GROUPS // 2
 CHUNK = 16
 POLLS = {5: (1, 2), 7: (3, 4, 5)}
-TURNS = {1: (6, 7, 8, 9), 2: (10, 11), 4: (12, 13, 14, 15)}
-JOIN, PART = 2, 6
+JOIN, MISSED, PART, ENDS = 2, 4, 6, 10
+TURNS = {1: (6, 7, 8, 9, 10, 11), PART: (12, 13, 14, 15)}
+SHIFT = 4.0
 
 ORDER = (
     (0, 0), (3, 0), (1, 0), (0, 3), (0, 1), (2, 0), (3, 3), (3, 1),
@@ -330,10 +331,10 @@
             old = m_s[j, rows, :]
             best = functools.reduce(jnp.maximum, cuts)
             top = jnp.maximum(
-                old, jnp.broadcast_to(jnp.max(best, axis=1, keepdims=True), (CHUNK, HD))
+                old, jnp.broadcast_to(jnp.max(best, axis=1, keepdims=True) - SHIFT, (CHUNK, HD))
             )
             for k, cut in enumerate(cuts):
-                weights[rows, k * HD : (k + 1) * HD] = jnp.exp2(cut - top).astype(BF16)
+                weights[rows, k * HD : (k + 1) * HD] = jnp.exp2((cut - top).astype(BF16))
             shrink = jnp.exp2(old - top)
             m_s[j, rows, :] = top
             acc[j, rows, 0:HD] = acc[j, rows, 0:HD] * shrink
@@ -383,7 +384,7 @@
             def _():
                 prepare(slot)
 
-    due = [i for i in range(PAIRS) if i < JOIN or i >= PART]
+    due = range(PAIRS // 2, PAIRS)
     wanted = [jnp.where(pair_at(i) < last // 2, 1, 0) for i in due]
     before = [sum(wanted[:k], jnp.int32(0)) for k in range(len(due))]
 
@@ -393,15 +394,21 @@
             for k in range(len(due))
         )
 
-    def turn(i, carry):
+    def turn(s, carry):
         for at, events in TURNS.items():
 
-            @pl.when(i == at)
+            @pl.when(s == at)
             def _():
                 for e in events:
                     arrive(ORDER[e])
 
-        @pl.when(i == JOIN)
+        i = jnp.where(s < MISSED, s, jnp.where(s < PART, s - MISSED, s - PART + PAIRS // 2))
+
+        @pl.when(s < MISSED)
+        def _():
+            prepare_pair(i)
+
+        @pl.when(s == JOIN)
         def _():
             for t in range(LENT):
                 for n in range(QN):
@@ -410,21 +417,23 @@
                     def _():
                         lend(t, n).wait_recv()
 
-        prepare_pair(i)
-
-        @pl.when(i == PART)
-        def _():
-            prepare_pair(PART + 1)
-
+        @pl.when((s == MISSED) & (taken > 0))
+        def _():
             def single(k, carry):
-                start = jnp.where(k == 2, 0, TILES)
-                odd = jnp.where(k == 2, g, last) % 2
-                n = jnp.where(k == 0, taken, odd * jnp.where(k == 1, taken, own))
-                block = jnp.where(k == 0, last, jnp.where(k == 1, last, g) - 1)
-                run(n, lambda t: (start + t, block, False), jnp.where(k == 0, 0, TOK))
+                block = last - k
+                prepare(block)
+                run(taken, lambda t: (TILES + t, block, False), k * TOK)
                 return carry
 
-            lax.fori_loop(0, 3, single, 0)
+            lax.fori_loop(0, 1 + last % 2, single, 0)
+
+        @pl.when(s == PART)
+        def _():
+            def rest(k, carry):
+                prepare_pair(k)
+                return carry
+
+            lax.fori_loop(PAIRS // 2, PAIRS, rest, 0)
 
             def away(j, carry):
                 run(before[-1] + wanted[-1], lambda t: (j, due_at(t), True))
@@ -439,15 +448,16 @@
                 return carry
 
             lax.fori_loop(TILES, TILES + taken, away, 0)
+            run(own * (g % 2), lambda t: (t, g - 1, False))
 
         two = pair_at(i)
-        joined = (i >= JOIN) & (i < PART) & (two < last // 2)
-        start = jnp.where(two < g // 2, 0, TILES)
-        stop = jnp.where(joined & low, TILES + taken, own)
+        join = (s >= JOIN) & (s < PART) & (two < last // 2)
+        start = jnp.where((two < g // 2) & ((s < MISSED) | (s >= PART)), 0, TILES)
+        stop = jnp.where(join & low, TILES + taken, jnp.where(start == 0, own, 0))
         run(jnp.maximum(stop - start, 0), lambda t: (start + t, two, True))
         return carry
 
-    lax.fori_loop(0, PAIRS, turn, 0)
+    lax.fori_loop(0, ENDS, turn, 0)
 
     for j in range(TILES):
 

time: 79.7 us -> 76.4 us (0.959)
  the two profiles are of different devices: /device:TPU:12 before, /device:TPU:30 now
where the time goes in v5:
time: 76.4 us; the launch traced here: 75.1 us
  Pallas kernels  74.3 us (97%)
  between operations  0.8 us (1%)
    pallas_call x1, Pallas kernels, per_device(): pl.pallas_call(prefill, out_shape=(jax.ShapeDtypeStruct((TOK, HEADS * HD)...  70 us
    pallas_call x1, Pallas kernels, per_device(): pl.pallas_call(decode, out_shape=(jax.ShapeDtypeStruct((TOK, HEADS * HD),...  4.25 us

profile of v5, /device:TPU:30, one launch (start us, length us, event | category | flops | bytes accessed | tf_op | source)
XLA Modules:
  0.0 75.1 jit_solution(6611364723044763016)
XLA Ops:
  0.6 70.0 %shard_map.104 = (bf16[512,1024]{1,0:T(8,128)(2,1)}, bf16[256,128]{1,0:T(8,128)(2,1)}, bf16[2,32,128]{2,1,0:T(8,128)(2,1)}, bf16[2,512,128]{2,1,0:T(8,128)(2,1)}) custom-call(bf16[512,8192]{1,0:T(8,128)(2,1)} %px.1, bf16[8192,1024]{1,0:T(8,128)(2,1)} %wq.1, bf16[8192,128]{1,0:T(8,128)(2,1)} %wk.1, bf16[8192,128]{1,0:T(8,128)(2,1)} %wv.1, ...), custom_call_target="tpu_custom_call" | custom-call | tf_op jit(solution)/shard_map/pallas_call | solution.py:579
  70.7 4.3 %shard_map.105 = (bf16[512,1024]{1,0:T(8,128)(2,1)}, bf16[32,1024]{1,0:T(8,128)(2,1)}) custom-call(s32[8,16]{1,0:T(8,128)} %table.1, s32[8]{0:T(128)} %lens.1, s32[1,32]{1,0:T(1,128)} %dest.1, bf16[512,1024]{1,0:T(8,128)(2,1)} %get-tuple-element.8.pre_in, bf16[4096,128]{1,0:T(8,128)(2,1)} %bitcast.3, bf16[256,128]{1,0:T(8,128)(2,1)} %get-tuple-element.9.dq, ...), custom_call_target="tpu_custom_call" | custom-call | tf_op jit(solution)/shard_map/pallas_call | solution.py:623

commit v6 on v5

--- a/solution.py
+++ b/solution.py
@@ -23,9 +23,8 @@
 STEPS = 4
 DEC = ROWS * STEPS
 ALL = TOK + DEC
-TILE_TOK = 64
-TILES = TOK // TILE_TOK
-TILE = TILE_TOK * HEADS
+TILES = HEADS
+TILE = TOK
 CACHE_ROWS = PAGES * PAGE * 2
 NEW_ROWS = 512
 SCALE = HD ** (-0.5) * 1.4426950408889634
@@ -40,7 +39,6 @@
 POLLS = {5: (1, 2), 7: (3, 4, 5)}
 JOIN, MISSED, PART, ENDS = 2, 4, 6, 10
 TURNS = {1: (6, 7, 8, 9, 10, 11), PART: (12, 13, 14, 15)}
-SHIFT = 4.0
 
 ORDER = (
     (0, 0), (3, 0), (1, 0), (0, 3), (0, 1), (2, 0), (3, 3), (3, 1),
@@ -196,30 +194,25 @@
             ).wait_recv()
         pass_on(event)
 
-    def lend(t, n):
-        rows = pl.ds(n * (TILE // QN), TILE // QN)
+    def lend(t):
         return pltpu.make_async_remote_copy(
-            src_ref=q_s.at[TILES - LENT + t, rows],
-            dst_ref=q_s.at[TILES + t + count - LENT, rows],
-            send_sem=qsend.at[t * QN + n],
-            recv_sem=qrecv.at[t * QN + n],
+            src_ref=q_s.at[t],
+            dst_ref=q_s.at[TILES + t],
+            send_sem=qsend.at[t],
+            recv_sem=qrecv.at[t],
             device_id=partner,
             device_id_type=MESH,
         )
 
-    def give_back(f):
-        at = pl.ds(pl.multiple_of((TILES - count + f) * TILE_TOK, TILE_TOK), TILE_TOK)
+    def give_back(t):
         return pltpu.make_async_remote_copy(
-            src_ref=of_s.at[f],
-            dst_ref=pre_out.at[at, :],
-            send_sem=osend.at[f],
-            recv_sem=orecv.at[f],
+            src_ref=of_s.at[t],
+            dst_ref=pre_out.at[:, pl.ds(t * HD, HD)],
+            send_sem=osend.at[t],
+            recv_sem=orecv.at[t],
             device_id=partner,
             device_id_type=MESH,
         )
-
-    def lent(t):
-        return count >= LENT - t
 
     def clear(j, carry):
         acc[j] = jnp.zeros((TILE, 2 * HD), F32)
@@ -281,18 +274,16 @@
                 arrive(ORDER[e])
         for hh in range(HEADS // QN):
             h = n * (HEADS // QN) + hh
-            for j in range(TILES):
-                q_s[j, h * TILE_TOK : (h + 1) * TILE_TOK, :] = (
-                    pacc[j * TILE_TOK : (j + 1) * TILE_TOK, hh * HD : (hh + 1) * HD] * SCALE
-                ).astype(BF16)
+            q_s[h] = (pacc[0:TOK, hh * HD : (hh + 1) * HD] * SCALE).astype(BF16)
             dq_out[h * DEC : (h + 1) * DEC, :] = (
                 pacc[TOK:ALL, hh * HD : (hh + 1) * HD] * SCALE
             ).astype(BF16)
-        for t in range(LENT):
-
-            @pl.when(jnp.logical_not(low) & lent(t))
-            def _():
-                lend(t, n).start()
+        if n == 0:
+            for t in range(LENT):
+
+                @pl.when(jnp.logical_not(low) & (t < count))
+                def _():
+                    lend(t).start()
 
     dkv = jnp.dot(x_s[TOK:ALL, :], wkv_s[...], preferred_element_type=F32)
     dkv_out[0] = dkv[:, 0:HD].astype(BF16)
@@ -316,7 +307,6 @@
     def absorb(item, buf, weights, ahead):
         j, two, side, width = part_of(item)
         if ahead is not None:
-            first = jnp.where(j < TILES, j, j - count) * TILE_TOK + ahead
             lead = lax.broadcasted_iota(jnp.int32, (CHUNK, HD), 1) - lax.broadcasted_iota(
                 jnp.int32, (CHUNK, HD), 0
             )
@@ -325,16 +315,21 @@
             cuts = [buf[rows, k * HD : (k + 1) * HD] for k in range(width // HD)]
             if ahead is not None:
                 cuts = [
-                    jnp.where(lead <= first + (c * CHUNK % TILE_TOK - k * HD), cut, LOW)
+                    jnp.where(lead <= c * CHUNK - k * HD + ahead, cut, LOW)
                     for k, cut in enumerate(cuts)
                 ]
+            if isinstance(ahead, int):
+                clear_from = (ahead + (c + 1) * CHUNK - 1) // HD + 1
+                for k in range(clear_from, len(cuts)):
+                    weights[rows, k * HD : (k + 1) * HD] = jnp.zeros((CHUNK, HD), BF16)
+                cuts = cuts[:clear_from]
             old = m_s[j, rows, :]
             best = functools.reduce(jnp.maximum, cuts)
             top = jnp.maximum(
-                old, jnp.broadcast_to(jnp.max(best, axis=1, keepdims=True) - SHIFT, (CHUNK, HD))
+                old, jnp.broadcast_to(jnp.max(best, axis=1, keepdims=True), (CHUNK, HD))
             )
             for k, cut in enumerate(cuts):
-                weights[rows, k * HD : (k + 1) * HD] = jnp.exp2((cut - top).astype(BF16))
+                weights[rows, k * HD : (k + 1) * HD] = jnp.exp2(cut - top).astype(BF16)
             shrink = jnp.exp2(old - top)
             m_s[j, rows, :] = top
             acc[j, rows, 0:HD] = acc[j, rows, 0:HD] * shrink
@@ -359,15 +354,15 @@
         def _():
             absorb(item(n - 1), sa_s, pa_s, ahead)
 
-    own = jnp.where(low, TILES, TILES - count)
+    first = jnp.where(low, 0, count)
+    own = TILES - first
     taken = jnp.where(low, count, 0)
 
     prepare(g)
-    run(own, lambda t: (t, g, False), 0)
-
-    def finish(j, h):
-        rows = slice(h * TILE_TOK, (h + 1) * TILE_TOK)
-        return (acc[j, rows, 0:HD] / acc[j, rows, HD:]).astype(BF16)
+    run(own, lambda t: (first + t, g, False), 0)
+
+    def finish(j):
+        return (acc[j, :, 0:HD] / acc[j, :, HD:]).astype(BF16)
 
     def pair_at(i):
         half = i // 4
@@ -411,11 +406,10 @@
         @pl.when(s == JOIN)
         def _():
             for t in range(LENT):
-                for n in range(QN):
-
-                    @pl.when(low & lent(t))
-                    def _():
-                        lend(t, n).wait_recv()
+
+                @pl.when(low & (t < count))
+                def _():
+                    lend(t).wait_recv()
 
         @pl.when((s == MISSED) & (taken > 0))
         def _():
@@ -437,8 +431,7 @@
 
             def away(j, carry):
                 run(before[-1] + wanted[-1], lambda t: (j, due_at(t), True))
-                for h in range(HEADS):
-                    of_s[j - TILES, :, h * HD : (h + 1) * HD] = finish(j, h)
+                of_s[j - TILES] = finish(j)
                 for f in range(LENT):
 
                     @pl.when(j == TILES + f)
@@ -448,12 +441,12 @@
                 return carry
 
             lax.fori_loop(TILES, TILES + taken, away, 0)
-            run(own * (g % 2), lambda t: (t, g - 1, False))
+            run(own * (g % 2), lambda t: (first + t, g - 1, False))
 
         two = pair_at(i)
         join = (s >= JOIN) & (s < PART) & (two < last // 2)
-        start = jnp.where((two < g // 2) & ((s < MISSED) | (s >= PART)), 0, TILES)
-        stop = jnp.where(join & low, TILES + taken, jnp.where(start == 0, own, 0))
+        start = jnp.where((two < g // 2) & ((s < MISSED) | (s >= PART)), first, TILES)
+        stop = jnp.where(join, TILES + taken, TILES)
         run(jnp.maximum(stop - start, 0), lambda t: (start + t, two, True))
         return carry
 
@@ -461,10 +454,9 @@
 
     for j in range(TILES):
 
-        @pl.when(j < own)
-        def _():
-            for h in range(HEADS):
-                pre_out[j * TILE_TOK : (j + 1) * TILE_TOK, h * HD : (h + 1) * HD] = finish(j, h)
+        @pl.when(j >= first)
+        def _():
+            pre_out[:, j * HD : (j + 1) * HD] = finish(j)
 
     mine = NEW_ROWS // GROUPS
     at = pl.ds(pl.multiple_of(g * mine, mine), mine)
@@ -478,13 +470,9 @@
         def _():
             give_back(t).wait_send()
 
-        @pl.when(lent(t) & jnp.logical_not(low))
-        def _():
-            for n in range(QN):
-                lend(t, n).wait_send()
-
         @pl.when((t < count) & jnp.logical_not(low))
         def _():
+            lend(t).wait_send()
             give_back(t).wait_recv()
 
     for k in range(1, 8):
@@ -593,7 +581,7 @@
             pltpu.VMEM((GROUPS, 2, TOK, HD), BF16),
             pltpu.VMEM((PAIRS, HD, 2 * TOK), BF16),
             pltpu.VMEM((PAIRS, 2 * TOK, 2 * HD), BF16),
-            pltpu.VMEM((LENT, TILE_TOK, HEADS * HD), BF16),
+            pltpu.VMEM((LENT, TOK, HD), BF16),
             pltpu.VMEM((TILES + LENT, TILE, HD), BF16),
             pltpu.VMEM((ALL, HEADS * HD // QN), F32),
             pltpu.VMEM((TILES + LENT, TILE, 2 * HD), F32),
@@ -611,8 +599,8 @@
             pltpu.SemaphoreType.DMA((7,)),
             pltpu.SemaphoreType.DMA((len(SENDS),)),
             pltpu.SemaphoreType.DMA((32,)),
-            pltpu.SemaphoreType.DMA((LENT * QN,)),
-            pltpu.SemaphoreType.DMA((LENT * QN,)),
+            pltpu.SemaphoreType.DMA((LENT,)),
+            pltpu.SemaphoreType.DMA((LENT,)),
             pltpu.SemaphoreType.DMA((LENT,)),
             pltpu.SemaphoreType.DMA((LENT,)),
         ],

time: 76.4 us -> 76.5 us (level); the launches traced: 75.1 us -> 76 us
  Pallas kernels: 74.3 us -> 75.2 us
    pallas_call x1, Pallas kernels: 70 us -> 71 us  [per_device(): pl.pallas_call(prefill, out_shape=(jax.ShapeDtypeStruct((TOK, HEADS * HD)...]
where the time goes in v6:
time: 76.5 us; the launch traced here: 76 us
  Pallas kernels  75.2 us (98%)
  between operations  0.8 us (1%)
    pallas_call x1, Pallas kernels, per_device(): pl.pallas_call(prefill, out_shape=(jax.ShapeDtypeStruct((TOK, HEADS * HD)...  71 us
    pallas_call x1, Pallas kernels, per_device(): pl.pallas_call(decode, out_shape=(jax.ShapeDtypeStruct((TOK, HEADS * HD),...  4.25 us

profile of v6, /device:TPU:30, one launch (start us, length us, event | category | flops | bytes accessed | tf_op | source)
XLA Modules:
  0.0 76.0 jit_solution(1172951254895678649)
XLA Ops:
  0.6 71.0 %shard_map.104 = (bf16[512,1024]{1,0:T(8,128)(2,1)}, bf16[256,128]{1,0:T(8,128)(2,1)}, bf16[2,32,128]{2,1,0:T(8,128)(2,1)}, bf16[2,512,128]{2,1,0:T(8,128)(2,1)}) custom-call(bf16[512,8192]{1,0:T(8,128)(2,1)} %px.1, bf16[8192,1024]{1,0:T(8,128)(2,1)} %wq.1, bf16[8192,128]{1,0:T(8,128)(2,1)} %wk.1, bf16[8192,128]{1,0:T(8,128)(2,1)} %wv.1, ...), custom_call_target="tpu_custom_call" | custom-call | tf_op jit(solution)/shard_map/pallas_call | solution.py:567
  71.6 4.3 %shard_map.105 = (bf16[512,1024]{1,0:T(8,128)(2,1)}, bf16[32,1024]{1,0:T(8,128)(2,1)}) custom-call(s32[8,16]{1,0:T(8,128)} %table.1, s32[8]{0:T(128)} %lens.1, s32[1,32]{1,0:T(1,128)} %dest.1, bf16[512,1024]{1,0:T(8,128)(2,1)} %get-tuple-element.8.pre_in, bf16[4096,128]{1,0:T(8,128)(2,1)} %bitcast.3, bf16[256,128]{1,0:T(8,128)(2,1)} %get-tuple-element.9.dq, ...), custom_call_target="tpu_custom_call" | custom-call | tf_op jit(solution)/shard_map/pallas_call | solution.py:611

commit v7 on v6

--- a/solution.py
+++ b/solution.py
@@ -29,14 +29,14 @@
 NEW_ROWS = 512
 SCALE = HD ** (-0.5) * 1.4426950408889634
 LOW = -1e30
-XC = 8
-QK = 4
-QN = 2
+XC = 4
+QK = 2
+QN = 4
 LENT = 4
-TAKES = (3, 3, 3, 3, 2, 2, 1, 0)
+TAKES = (3, 3, 2, 2, 1, 1, 1, 0)
 PAIRS = GROUPS // 2
 CHUNK = 16
-POLLS = {5: (1, 2), 7: (3, 4, 5)}
+POLLS = {2: (1, 2), 3: (3, 4, 5)}
 JOIN, MISSED, PART, ENDS = 2, 4, 6, 10
 TURNS = {1: (6, 7, 8, 9, 10, 11), PART: (12, 13, 14, 15)}
 
@@ -116,7 +116,7 @@
 
     def q_copy(n, k):
         rows = pl.ds(k * (D // QK), D // QK)
-        cols = pl.ds(n * (HEADS * HD // QN), HEADS * HD // QN)
+        cols = pl.ds(pl.multiple_of(n * (HEADS * HD // QN), HEADS * HD // QN), HEADS * HD // QN)
         return pltpu.make_async_copy(wq.at[rows, cols], wq_s.at[rows, cols], qsem.at[n * QK + k])
 
     my_cols = pl.ds(pl.multiple_of(tensor * (D // 8), D // 8), D // 8)
@@ -232,7 +232,7 @@
         w_copy(c, wv, HD, wvsem).wait()
         for k in range(QN * QK):
 
-            @pl.when(c == 4 + k // 2)
+            @pl.when(c == 2 + k // 4)
             def _():
                 q_copy(k // QK, k % QK).start()
 
@@ -259,32 +259,39 @@
         dec_arrival(k).wait_recv()
 
     width = HEADS * HD // QN
-    for n in range(QN):
+
+    def query_step(n, carry):
         for k in range(QK):
             q_copy(n, k).wait()
-            at = slice(k * (D // QK), (k + 1) * (D // QK))
-            part = jnp.dot(
-                x_s[:, at], wq_s[at, n * width : (n + 1) * width], preferred_element_type=F32
-            )
-            if k == 0:
-                pacc[...] = part
-            else:
-                pacc[...] += part
-            for e in POLLS.get(n * QK + k, ()):
-                arrive(ORDER[e])
+        part = jnp.dot(
+            x_s[...],
+            wq_s[:, pl.ds(pl.multiple_of(n * width, width), width)],
+            preferred_element_type=F32,
+        )
         for hh in range(HEADS // QN):
             h = n * (HEADS // QN) + hh
-            q_s[h] = (pacc[0:TOK, hh * HD : (hh + 1) * HD] * SCALE).astype(BF16)
-            dq_out[h * DEC : (h + 1) * DEC, :] = (
-                pacc[TOK:ALL, hh * HD : (hh + 1) * HD] * SCALE
-            ).astype(BF16)
-        if n == 0:
+            scaled = (part[:, hh * HD : (hh + 1) * HD] * SCALE).astype(BF16)
+            q_s[h] = scaled[0:TOK]
+            dq_out[pl.ds(pl.multiple_of(h * DEC, DEC), DEC), :] = scaled[TOK:ALL]
+
+        @pl.when(n == QN // 2 - 1)
+        def _():
             for t in range(LENT):
 
                 @pl.when(jnp.logical_not(low) & (t < count))
                 def _():
                     lend(t).start()
 
+        for at, events in POLLS.items():
+
+            @pl.when(n == at)
+            def _():
+                for e in events:
+                    arrive(ORDER[e])
+
+        return carry
+
+    lax.fori_loop(0, QN, query_step, 0)
     dkv = jnp.dot(x_s[TOK:ALL, :], wkv_s[...], preferred_element_type=F32)
     dkv_out[0] = dkv[:, 0:HD].astype(BF16)
     dkv_out[1] = dkv[:, HD : 2 * HD].astype(BF16)
@@ -344,7 +351,11 @@
         def two(t, carry):
             score(item(2 * t + 1), sb_s)
             absorb(item(2 * t), sa_s, pa_s, ahead)
-            score(item(jnp.minimum(2 * t + 2, n - 1)), sa_s)
+
+            @pl.when(2 * t + 2 < n)
+            def _():
+                score(item(2 * t + 2), sa_s)
+
             absorb(item(2 * t + 1), sb_s, pb_s, ahead)
             return carry
 
@@ -583,7 +594,7 @@
             pltpu.VMEM((PAIRS, 2 * TOK, 2 * HD), BF16),
             pltpu.VMEM((LENT, TOK, HD), BF16),
             pltpu.VMEM((TILES + LENT, TILE, HD), BF16),
-            pltpu.VMEM((ALL, HEADS * HD // QN), F32),
+            pltpu.VMEM((TOK, 2 * HD), F32),
             pltpu.VMEM((TILES + LENT, TILE, 2 * HD), F32),
             pltpu.VMEM((TILES + LENT, TILE, HD), F32),
             pltpu.VMEM((TILE, 2 * TOK), F32),

time: 76.5 us -> 82.1 us (1.073)
  the two profiles are of different devices: /device:TPU:30 before, /device:TPU:23 now
where the time goes in v7:
time: 82.1 us; the launch traced here: 81.9 us
  Pallas kernels  81.1 us (99%)
    pallas_call x1, Pallas kernels, per_device(): pl.pallas_call(prefill, out_shape=(jax.ShapeDtypeStruct((TOK, HEADS * HD)...  76.9 us
    pallas_call x1, Pallas kernels, per_device(): pl.pallas_call(decode, out_shape=(jax.ShapeDtypeStruct((TOK, HEADS * HD),...  4.25 us

profile of v7, /device:TPU:23, one launch (start us, length us, event | category | flops | bytes accessed | tf_op | source)
XLA Modules:
  0.0 81.9 jit_solution(589645341531465874)
XLA Ops:
  0.6 76.9 %shard_map.104 = (bf16[512,1024]{1,0:T(8,128)(2,1)}, bf16[256,128]{1,0:T(8,128)(2,1)}, bf16[2,32,128]{2,1,0:T(8,128)(2,1)}, bf16[2,512,128]{2,1,0:T(8,128)(2,1)}) custom-call(bf16[512,8192]{1,0:T(8,128)(2,1)} %px.1, bf16[8192,1024]{1,0:T(8,128)(2,1)} %wq.1, bf16[8192,128]{1,0:T(8,128)(2,1)} %wk.1, bf16[8192,128]{1,0:T(8,128)(2,1)} %wv.1, ...), custom_call_target="tpu_custom_call" | custom-call | tf_op jit(solution)/shard_map/pallas_call | solution.py:578
  77.5 4.3 %shard_map.105 = (bf16[512,1024]{1,0:T(8,128)(2,1)}, bf16[32,1024]{1,0:T(8,128)(2,1)}) custom-call(s32[8,16]{1,0:T(8,128)} %table.1, s32[8]{0:T(128)} %lens.1, s32[1,32]{1,0:T(1,128)} %dest.1, bf16[512,1024]{1,0:T(8,128)(2,1)} %get-tuple-element.8.pre_in, bf16[4096,128]{1,0:T(8,128)(2,1)} %bitcast.3, bf16[256,128]{1,0:T(8,128)(2,1)} %get-tuple-element.9.dq, ...), custom_call_target="tpu_custom_call" | custom-call | tf_op jit(solution)/shard_map/pallas_call | solution.py:622

commit v8 on v7

--- a/solution.py
+++ b/solution.py
@@ -33,7 +33,7 @@
 QK = 2
 QN = 4
 LENT = 4
-TAKES = (3, 3, 2, 2, 1, 1, 1, 0)
+TAKES = (3, 3, 3, 2, 2, 1, 1, 0)
 PAIRS = GROUPS // 2
 CHUNK = 16
 POLLS = {2: (1, 2), 3: (3, 4, 5)}
@@ -309,15 +309,25 @@
 
     def score(item, buf):
         j, two, side, width = part_of(item)
-        buf[:, 0:width] = jnp.dot(q_s[j], kt_s[two, :, side], preferred_element_type=F32)
-
-    def absorb(item, buf, weights, ahead):
+        at = 0 if width == 2 * TOK else pl.multiple_of((item[1] % 2) * TOK, TOK)
+
+        def step(n):
+            keys = kt_s[two, :, pl.ds(at + n * 2 * HD, 2 * HD)]
+            buf[:, n * 2 * HD : (n + 1) * 2 * HD] = jnp.dot(
+                q_s[j], keys, preferred_element_type=F32
+            )
+
+        return [functools.partial(step, n) for n in range(width // (2 * HD))]
+
+    def absorb(item, buf, weights, ahead, beside=()):
         j, two, side, width = part_of(item)
         if ahead is not None:
             lead = lax.broadcasted_iota(jnp.int32, (CHUNK, HD), 1) - lax.broadcasted_iota(
                 jnp.int32, (CHUNK, HD), 0
             )
         for c in range(TILE // CHUNK):
+            if beside and c % (TILE // CHUNK // len(beside)) == 0:
+                beside[c // (TILE // CHUNK // len(beside))]()
             rows = slice(c * CHUNK, (c + 1) * CHUNK)
             cuts = [buf[rows, k * HD : (k + 1) * HD] for k in range(width // HD)]
             if ahead is not None:
@@ -346,17 +356,13 @@
     def run(n, item, ahead=None):
         @pl.when(n > 0)
         def _():
-            score(item(0), sa_s)
+            for step in score(item(0), sa_s):
+                step()
 
         def two(t, carry):
-            score(item(2 * t + 1), sb_s)
-            absorb(item(2 * t), sa_s, pa_s, ahead)
-
-            @pl.when(2 * t + 2 < n)
-            def _():
-                score(item(2 * t + 2), sa_s)
-
-            absorb(item(2 * t + 1), sb_s, pb_s, ahead)
+            now, later, last_one = item(2 * t), item(2 * t + 1), item(jnp.minimum(2 * t + 2, n - 1))
+            absorb(now, sa_s, pa_s, ahead, score(later, sb_s))
+            absorb(later, sb_s, pb_s, ahead, score(last_one, sa_s))
             return carry
 
         lax.fori_loop(0, n // 2, two, 0)

time: 82.1 us -> 75.6 us (0.921)
  the two profiles are of different devices: /device:TPU:23 before, /device:TPU:30 now
where the time goes in v8:
time: 75.6 us; the launch traced here: 75.5 us
  Pallas kernels  74.7 us (99%)
  between operations  0.8 us (1%)
    pallas_call x1, Pallas kernels, per_device(): pl.pallas_call(prefill, out_shape=(jax.ShapeDtypeStruct((TOK, HEADS * HD)...  70.4 us
    pallas_call x1, Pallas kernels, per_device(): pl.pallas_call(decode, out_shape=(jax.ShapeDtypeStruct((TOK, HEADS * HD),...  4.25 us

profile of v8, /device:TPU:30, one launch (start us, length us, event | category | flops | bytes accessed | tf_op | source)
XLA Modules:
  0.0 75.5 jit_solution(15847385328107571347)
XLA Ops:
  0.6 70.4 %shard_map.104 = (bf16[512,1024]{1,0:T(8,128)(2,1)}, bf16[256,128]{1,0:T(8,128)(2,1)}, bf16[2,32,128]{2,1,0:T(8,128)(2,1)}, bf16[2,512,128]{2,1,0:T(8,128)(2,1)}) custom-call(bf16[512,8192]{1,0:T(8,128)(2,1)} %px.1, bf16[8192,1024]{1,0:T(8,128)(2,1)} %wq.1, bf16[8192,128]{1,0:T(8,128)(2,1)} %wk.1, bf16[8192,128]{1,0:T(8,128)(2,1)} %wv.1, ...), custom_call_target="tpu_custom_call" | custom-call | tf_op jit(solution)/shard_map/pallas_call | solution.py:584
  71.1 4.3 %shard_map.105 = (bf16[512,1024]{1,0:T(8,128)(2,1)}, bf16[32,1024]{1,0:T(8,128)(2,1)}) custom-call(s32[8,16]{1,0:T(8,128)} %table.1, s32[8]{0:T(128)} %lens.1, s32[1,32]{1,0:T(1,128)} %dest.1, bf16[512,1024]{1,0:T(8,128)(2,1)} %get-tuple-element.8.pre_in, bf16[4096,128]{1,0:T(8,128)(2,1)} %bitcast.3, bf16[256,128]{1,0:T(8,128)(2,1)} %get-tuple-element.9.dq, ...), custom_call_target="tpu_custom_call" | custom-call | tf_op jit(solution)/shard_map/pallas_call | solution.py:628

commit v9 on v8

--- a/solution.py
+++ b/solution.py
@@ -499,9 +499,9 @@
 
 
 def decode(
-    table, lens, dest, pre_in, cache, dq, dkv, new,
+    table, lens, dest, pre_in, cache, dq_in, dkv_in, new_in,
     pre_out, dec_out,
-    pre_s, pool_s, mix_s, page_s, dq_s, out_s, in_sem, out_sem, pool_sem,
+    dq, dkv, new, pre_s, pool_s, mix_s, page_s, dq_s, out_s, in_sem, out_sem, pool_sem, small_sem,
 ):
     half = TOK // 2
 
@@ -514,16 +514,26 @@
         return pltpu.make_async_copy(pre_s.at[rows, :], pre_out.at[rows, :], out_sem.at[k])
 
     pool = pltpu.make_async_copy(cache, page_s, pool_sem)
+    small = [
+        pltpu.make_async_copy(src, dst, small_sem.at[k])
+        for k, (src, dst) in enumerate(((new_in, new), (dq_in, dq), (dkv_in, dkv)))
+    ]
+    small[0].start()
     pool.start()
+    small[1].start()
+    small[2].start()
     for k in range(2):
         take(k).start()
 
+    small[0].wait()
     mix_s[pl.ds(0, NEW_ROWS, stride=2), :] = new[0].astype(F32)
     mix_s[pl.ds(1, NEW_ROWS, stride=2), :] = new[1].astype(F32)
     pool.wait()
     for m in range(TOK // PAGE):
         at = pl.ds(pl.multiple_of(dest[0, m] * 2 * PAGE, 2 * PAGE), 2 * PAGE)
         page_s[at, :] = mix_s[m * 2 * PAGE : (m + 1) * 2 * PAGE, :].astype(BF16)
+    small[1].wait()
+    small[2].wait()
     dq_s[...] = dq[...].astype(F32)
     for r in range(ROWS):
         for j in range(MAXP):
@@ -631,9 +641,12 @@
             jax.ShapeDtypeStruct((TOK, HEADS * HD), BF16),
             jax.ShapeDtypeStruct((DEC, HEADS * HD), BF16),
         ),
-        in_specs=[smem] * 3 + [hbm] * 2 + [vmem] * 3,
+        in_specs=[smem] * 3 + [hbm] * 5,
         out_specs=(hbm, vmem),
         scratch_shapes=[
+            pltpu.VMEM((HEADS * DEC, HD), BF16),
+            pltpu.VMEM((2, DEC, HD), BF16),
+            pltpu.VMEM((2, NEW_ROWS, HD), BF16),
             pltpu.VMEM((TOK, HEADS * HD), BF16),
             pltpu.VMEM((ROWS, 2 * MAXP * PAGE, HD), BF16),
             pltpu.VMEM((2 * NEW_ROWS, HD), F32),
@@ -643,6 +656,7 @@
             pltpu.SemaphoreType.DMA((2,)),
             pltpu.SemaphoreType.DMA((2,)),
             pltpu.SemaphoreType.DMA,
+            pltpu.SemaphoreType.DMA((3,)),
         ],
         compiler_params=pltpu.CompilerParams(vmem_limit_bytes=63 * 1024 * 1024),
     )(page_table, lengths, dest_slots, pre, cache.reshape(CACHE_ROWS, HD), dq, dkv, new)

time: 75.6 us -> 75.5 us (level)
  no operation moved by 1% of the time
where the time goes in v9:
time: 75.5 us; the launch traced here: 75.4 us
  Pallas kernels  74.6 us (99%)
  between operations  0.8 us (1%)
    pallas_call x1, Pallas kernels, per_device(): pl.pallas_call(prefill, out_shape=(jax.ShapeDtypeStruct((TOK, HEADS * HD)...  70.4 us
    pallas_call x1, Pallas kernels, per_device(): pl.pallas_call(decode, out_shape=(jax.ShapeDtypeStruct((TOK, HEADS * HD),...  4.13 us

profile of v9, /device:TPU:30, one launch (start us, length us, event | category | flops | bytes accessed | tf_op | source)
XLA Modules:
  0.0 75.4 jit_solution(3443623905226188076)
XLA Ops:
  0.6 70.4 %shard_map.104 = (bf16[512,1024]{1,0:T(8,128)(2,1)}, bf16[256,128]{1,0:T(8,128)(2,1)}, bf16[2,32,128]{2,1,0:T(8,128)(2,1)}, bf16[2,512,128]{2,1,0:T(8,128)(2,1)}) custom-call(bf16[512,8192]{1,0:T(8,128)(2,1)} %px.1, bf16[8192,1024]{1,0:T(8,128)(2,1)} %wq.1, bf16[8192,128]{1,0:T(8,128)(2,1)} %wk.1, bf16[8192,128]{1,0:T(8,128)(2,1)} %wv.1, ...), custom_call_target="tpu_custom_call" | custom-call | tf_op jit(solution)/shard_map/pallas_call | solution.py:594
  71.1 4.1 %shard_map.105 = (bf16[512,1024]{1,0:T(8,128)(2,1)}, bf16[32,1024]{1,0:T(8,128)(2,1)}) custom-call(s32[8,16]{1,0:T(8,128)} %table.1, s32[8]{0:T(128)} %lens.1, s32[1,32]{1,0:T(1,128)} %dest.1, bf16[512,1024]{1,0:T(8,128)(2,1)} %get-tuple-element.8.pre_in, bf16[4096,128]{1,0:T(8,128)(2,1)} %bitcast.3, bf16[256,128]{1,0:T(8,128)(2,1)} %get-tuple-element.9.dq_in, ...), custom_call_target="tpu_custom_call" | custom-call | tf_op jit(solution)/shard_map/pallas_call | solution.py:638
